TPU v7x, 256 devices: a whole 4x4x8 slice. The times are simulated.
256 devices in a mesh: box: 64 (over x, z, core), ch: 4 (over y).
Axes of the slice: x: 4, y: 4, z: 8, core: 2. Of those that a mesh axis runs over, the one named last changes fastest.
Arguments:
- features: bfloat16 [256, 262144], P('ch', 'box'), may hold values from -6 to 6
- occupied: int32 [262144], P('box'), may hold values 0 or 1
- send_lists: int32 [64, 2, 8], P('box'), may hold values from 0 to 32, as said below
- kernel_map: int32 [64, 27, 32], P('box'), may hold values from 0 to 48, as said below
- weights: bfloat16 [27, 256, 256], P(None, 'ch'), may hold values from -0.078125 to 0.078125
- norm_gain: float32 [256], P('ch'), may hold values from 0.25 to 1.75
- norm_shift: float32 [256], P('ch'), may hold values from -3 to 3
- out_grad: bfloat16 [256, 262144], P('ch', 'box'), may hold values from -6 to 6
Outputs:
- out_features: bfloat16 [256, 262144], P('ch', 'box')
- in_grad: bfloat16 [256, 262144], P('ch', 'box')
- weight_grad: float32 [27, 256, 256], P(None, 'ch')
- gain_grad: float32 [256], P('ch')
- shift_grad: float32 [256], P('ch')
Inputs may be any that keep to these rules, and one draw needn't show every extreme that they name: `send_lists`: each entry names a local block, or 32 for an empty slot; the first slot of box 0's list to the lower box is empty and the first slot of its list to the upper box is block 0. `kernel_map`: each entry indexes the extended blocks; 48 is the zero block; offset 13 maps every block to itself.
All inputs are finite; a program needn't handle non-finite values. No bound on the sum of `occupied` on one device may be relied on, other than what follows from the above.
Results may differ from a plain program's by a relative error of at most 0.01295.
Values may be sent and summed in bfloat16 or wider, within the bound.
A program may use at most 64 MiB of HBM per device.

v0:
```python
import jax
import jax.numpy as jnp
from jax import lax
from jax.sharding import PartitionSpec as P

BLOCK = 128


def shifted_2(block, axis, distance):
    devices = range(lax.axis_size(axis))
    route = [(i - distance, i) for i in devices if i - distance in devices]
    return lax.ppermute(block, axis, route)


def per_device(
    features, occupied, send_lists, kernel_map, weights, norm_gain, norm_shift, out_grad
):
    local_ch, row_count = features.shape
    blocks = row_count // BLOCK
    slots = send_lists.shape[2]
    full_ch = weights.shape[2]
    occupancy = occupied.astype(jnp.float32)[None, :]
    masked = features * occupied.astype(jnp.bfloat16)[None, :]
    local_blocks = masked.reshape(local_ch, blocks, BLOCK)
    send_picks = send_lists[0]
    offset_table = kernel_map[0]
    padded_local = jnp.concatenate(
        [local_blocks, jnp.zeros((local_ch, 1, BLOCK), jnp.bfloat16)], axis=1
    )
    whole = lax.all_gather(padded_local, "ch", axis=0, tiled=True)
    from_below = shifted_2(whole[:, send_picks[1]], "box", 1)
    from_above = shifted_2(whole[:, send_picks[0]], "box", -1)
    extended = jnp.concatenate(
        [whole[:, :blocks], from_below, from_above, jnp.zeros((full_ch, 1, BLOCK), jnp.bfloat16)],
        axis=1,
    )
    ext_count = extended.shape[1]

    def conv_step(running, step_inputs):
        source_row, kernel_slab = step_inputs
        gathered = extended[:, source_row].reshape(full_ch, row_count)
        return (running + jnp.dot(kernel_slab, gathered, preferred_element_type=jnp.float32), None)

    conv, _ = lax.scan(
        conv_step, jnp.zeros((local_ch, row_count), jnp.float32), (offset_table, weights)
    )
    first_sum, second_sum, voxel_count = lax.psum(
        (
            jnp.sum(occupancy * conv, axis=1),
            jnp.sum(occupancy * conv * conv, axis=1),
            jnp.sum(occupancy),
        ),
        "box",
    )
    stat_mean = first_sum / voxel_count
    stat_var = second_sum / voxel_count - stat_mean * stat_mean
    inv_std = (1.0 / jnp.sqrt(stat_var + 1e-05))[:, None]
    normed = (conv - stat_mean[:, None]) * inv_std
    gain_col = norm_gain[:, None]
    shifted = normed * gain_col + norm_shift[:, None]
    out_features = (occupancy * jnp.maximum(shifted, 0.0)).astype(jnp.bfloat16)
    relu_grad = occupancy * out_grad.astype(jnp.float32) * (shifted > 0.0).astype(jnp.float32)
    shift_grad, gain_grad = lax.psum(
        (jnp.sum(relu_grad, axis=1), jnp.sum(relu_grad * normed, axis=1)), "box"
    )
    conv_grad = (
        occupancy
        * inv_std
        * gain_col
        * (
            relu_grad
            - shift_grad[:, None] / voxel_count
            - normed * gain_grad[:, None] / voxel_count
        )
    ).astype(jnp.bfloat16)

    def back_step(running, step_inputs):
        source_row, kernel_slab = step_inputs
        gathered = extended[:, source_row].reshape(full_ch, row_count)
        kernel_term = lax.dot_general(
            conv_grad, gathered, (((1,), (1,)), ((), ())), preferred_element_type=jnp.float32
        )
        contrib = lax.dot_general(
            kernel_slab, conv_grad, (((0,), (0,)), ((), ())), preferred_element_type=jnp.float32
        )
        running = running.at[:, source_row].add(contrib.reshape(full_ch, blocks, BLOCK))
        return (running, kernel_term)

    ext_grad, kernel_terms = lax.scan(
        back_step, jnp.zeros((full_ch, ext_count, BLOCK), jnp.float32), (offset_table, weights)
    )
    weight_grad = lax.psum(kernel_terms, "box")
    reduced = lax.psum_scatter(ext_grad, "ch", scatter_dimension=0, tiled=True)
    to_lower = shifted_2(reduced[:, blocks : blocks + slots], "box", -1)
    to_upper = shifted_2(reduced[:, blocks + slots : blocks + 2 * slots], "box", 1)
    padded_grad = jnp.concatenate(
        [reduced[:, :blocks], jnp.zeros((local_ch, 1, BLOCK), jnp.float32)], axis=1
    )
    padded_grad = padded_grad.at[:, send_picks[1]].add(to_lower).at[:, send_picks[0]].add(to_upper)
    input_grad = padded_grad[:, :blocks]
    in_grad = (occupancy * input_grad.reshape(local_ch, row_count)).astype(jnp.bfloat16)
    return (out_features, in_grad, weight_grad, gain_grad, shift_grad)


def solution(mesh):
    in_specs = (
        P("ch", "box"),
        P("box"),
        P("box", None, None),
        P("box", None, None),
        P(None, "ch", None),
        P("ch"),
        P("ch"),
        P("ch", "box"),
    )
    out_specs = (P("ch", "box"), P("ch", "box"), P(None, "ch", None), P("ch"), P("ch"))
    return jax.shard_map(
        per_device, mesh=mesh, in_specs=in_specs, out_specs=out_specs, check_vma=False
    )
```

profile of v0, /device:TPU:1, one launch (start us, length us, event | category | flops | bytes accessed | tf_op | source)
XLA Modules:
  0.0 1422.1 jit_solution(3726860164791932928)
XLA Ops:
  10.2 38.0 %all-gather.2.cloned.1.call-done = bf16[256,33,128]{2,0,1:T(8,128)(2,1)} async-done(((bf16[64,33,128]{2,0,1:T(8,128)(2,1)}), bf16[256,33,128]{2,0,1:T(8,128)(2,1)}) %all-gather.2.cloned.1.call-update) | async-done | bytes 2162704 | tf_op jit(solution)/shard_map/all_gather | solution.py:30
  60.3 6.7 collective-permute-done.1
  69.0 242.1 %while.24 = (s32[]{:T(128)}, f32[64,4096]{1,0:T(8,128)S(1)}, bf16[27,64,256]{2,1,0:T(8,128)(2,1)}, s32[27,32]{1,0:T(8,128)S(1)}, bf16[256,49,128]{2,0,1:T(8,128)(2,1)}, /*index=5*/s32[]{:T(128)}, s32[]{:T(128)}) while((s32[]{:T(128)}, f32[64,4096]{1,0:T(8,128)S(1)}, bf16[27,64,256]{2,1,0:T(8,128)(2,1)}, s32[27,32]{1,0:T(8,128)S(1)}, ...), condition=%wide.region_1.2_spmd.clone, body=%wide.region_0.1_spmd.clone.sunk | while | flops 134743136 | bytes 12620391 | solution.py:44
  69.0 4.1 gather_fusion.1
  311.4 123.2 %all-reduce.2 = (f32[64]{0:T(128)S(1)}, f32[]{:T(128)}, f32[64]{0:T(128)S(1)}) all-reduce(f32[64]{0:T(128)S(1)} %get-tuple-element.92, f32[]{:T(128)} %convert_reduce_fusion, f32[64]{0:T(128)S(1)} %get-tuple-element.91), channel_id=1, replica_groups=mesh['box'=64,'ch'=4] {'box'}, use_global_device_ids=true, to_apply=%region_3.4 | all-reduce | flops 129 | bytes 1032 | tf_op jit(solution)/shard_map/psum | solution.py:47
  437.7 125.4 %all-reduce.1 = (f32[64]{0:T(128)S(1)}, f32[64]{0:T(128)S(1)}) all-reduce(f32[64]{0:T(128)S(1)} %get-tuple-element.94, f32[64]{0:T(128)S(1)} %get-tuple-element.93), channel_id=1, replica_groups=mesh['box'=64,'ch'=4] {'box'}, use_global_device_ids=true, to_apply=%region_11.12 | all-reduce | flops 128 | bytes 1024 | tf_op jit(solution)/shard_map/psum | solution.py:63
  569.1 594.3 %while.23 = (s32[]{:T(128)}, f32[256,49,128]{2,0,1:T(8,128)}, f32[27,64,256]{2,1,0:T(8,128)}, s32[27,32]{1,0:T(8,128)S(1)}, bf16[27,64,256]{2,1,0:T(8,128)(2,1)}...) while((s32[]{:T(128)}, f32[256,49,128]{2,0,1:T(8,128)}, ...), condition=%wide.region_14.15_spmd, body=%wide.region_12.14_spmd.sunk | while | flops 269485152 | bytes 28414696 | solution.py:89
  569.1 4.1 gather_fusion
  581.1 10.1 scatter_fusion
  591.2 4.1 gather_fusion
  603.2 10.0 scatter_fusion
  613.3 4.1 gather_fusion
  625.2 10.0 scatter_fusion
  635.2 4.1 gather_fusion
  647.2 10.0 scatter_fusion
  657.2 4.1 gather_fusion
  669.2 9.9 scatter_fusion
  679.1 4.1 gather_fusion
  691.1 10.0 scatter_fusion
  701.1 4.1 gather_fusion
  713.1 10.0 scatter_fusion
  723.1 4.1 gather_fusion
  735.0 9.9 scatter_fusion
  744.9 4.1 gather_fusion
  756.9 9.9 scatter_fusion
  766.9 4.1 gather_fusion
  778.8 10.1 scatter_fusion
  789.0 4.1 gather_fusion
  801.0 10.0 scatter_fusion
  811.0 4.1 gather_fusion
  823.0 10.1 scatter_fusion
  833.0 4.1 gather_fusion
  845.0 10.0 scatter_fusion
  855.1 4.1 gather_fusion
  867.0 10.2 scatter_fusion
  877.2 4.1 gather_fusion
  889.2 10.1 scatter_fusion
  899.3 4.1 gather_fusion
  911.2 9.9 scatter_fusion
  921.1 4.1 gather_fusion
  933.1 10.1 scatter_fusion
  943.2 4.1 gather_fusion
  955.1 9.9 scatter_fusion
  965.1 4.1 gather_fusion
  977.0 10.0 scatter_fusion
  987.1 4.1 gather_fusion
  999.1 10.0 scatter_fusion
  1009.1 4.1 gather_fusion
  1021.1 10.0 scatter_fusion
  1031.1 4.1 gather_fusion
  1043.1 10.0 scatter_fusion
  1053.1 4.1 gather_fusion
  1065.1 10.1 scatter_fusion
  1075.2 4.1 gather_fusion
  1087.2 10.1 scatter_fusion
  1097.2 4.1 gather_fusion
  1109.2 10.1 scatter_fusion
  1119.3 4.1 gather_fusion
  1131.3 10.1 scatter_fusion
  1141.4 4.1 gather_fusion
  1153.4 10.0 scatter_fusion
  1164.1 59.0 %reduce-scatter.2.cloned.1.call-done = f32[64,49,128]{2,0,1:T(8,128)} async-done(((f32[256,49,128]{2,0,1:T(8,128)}), f32[64,49,128]{2,0,1:T(8,128)}) %reduce-scatter.2.cloned.1.call-update) | async-done | bytes 1605648 | tf_op jit(solution)/shard_map/reduce_scatter | solution.py:93
  1231.2 4.4 collective-permute-done.2
  1238.2 174.4 %all-reduce.5.cloned.1.call-done = f32[27,64,256]{2,1,0:T(8,128)} async-done(((f32[27,64,256]{2,1,0:T(8,128)}), f32[27,64,256]{2,1,0:T(8,128)}) %all-reduce.5.cloned.1.call-update) | async-done | bytes 1769488 | tf_op jit(solution)/shard_map/psum | solution.py:92
  (328 shorter events, 490.6 us)
Async XLA Ops:
  7.2 3.0 copy-start.5
  7.2 41.0 %all-gather.2.cloned.1.call-start = ((), (), s32[]{:S(2)}) async-start(), calls=%async_computation.1 | async-start | bytes 2703360 | tf_op jit(solution)/shard_map/all_gather | solution.py:30
  9.2 49.2 %copy-start.3 = (s32[1,27,32]{2,0,1:T(1,128)S(1)}, s32[1,27,32]{2,0,1:T(1,128)}, u32[]{:S(2)}) copy-start(s32[1,27,32]{2,0,1:T(1,128)} %param.15) | copy-start | bytes 10372
  9.2 49.3 %copy-start.2 = (s32[4096]{0:T(1024)S(1)}, s32[4096]{0:T(1024)}, u32[]{:S(2)}) copy-start(s32[4096]{0:T(1024)} %param.13) | copy-start | bytes 49156
  10.1 1213.0 %reduce-scatter.2.cloned.1.call-start = ((), (), s32[]{:S(2)}) async-start(), calls=%async_computation.2 | async-start | bytes 8028160 | tf_op jit(solution)/shard_map/reduce_scatter | solution.py:93
  50.4 9.9 collective-permute-start
  56.5 10.5 collective-permute-start.1
  59.1 7.9 slice-start
  69.0 366.1 %copy-start.4 = (f32[64]{0:T(128)S(1)}, f32[64]{0:T(128)}, u32[]{:S(2)}) copy-start(f32[64]{0:T(128)} %param.17) | copy-start | bytes 772
  69.0 366.1 %copy-start.6 = (f32[64]{0:T(128)S(1)}, f32[64]{0:T(128)}, u32[]{:S(2)}) copy-start(f32[64]{0:T(128)} %param.18) | copy-start | bytes 772
  311.1 252.6 %copy-start.1 = (bf16[64,4096]{1,0:T(8,128)(2,1)S(1)}, bf16[64,4096]{1,0:T(8,128)(2,1)}, u32[]{:S(2)}) copy-start(bf16[64,4096]{1,0:T(8,128)(2,1)} %param.19) | copy-start | bytes 1572868
  563.1 6.0 copy-start.8
  563.1 6.0 copy-start.9
  565.6 3.5 copy-start
  1163.4 66.4 %copy-start.7 = (pred[33]{0:T(512)(128)(4,1)S(1)}, pred[33]{0:T(512)(128)(4,1)}, u32[]{:S(2)}) copy-start(pred[33]{0:T(512)(128)(4,1)} %constant.27.clone.1) | copy-start | bytes 103
  1163.4 249.3 %all-reduce.5.cloned.1.call-start = ((), (), s32[]{:S(2)}) async-start(), calls=%async_computation.3 | async-start | bytes 3538944 | tf_op jit(solution)/shard_map/psum | solution.py:92
  1224.2 12.3 collective-permute-start.3
  1227.9 7.7 collective-permute-start.2
Sparse Core Ops, SparseCore 0:
  10.4 37.7 all-gather.1
  1163.5 59.5 reduce-scatter.1
  1227.1 185.5 all-reduce.4
where the time goes:
time: 1430 us; the launch traced here: 1420 us
  local copies, waits for them, and re-layouts  409 us (29%)
  other arithmetic  286 us (20%)
  waiting for transfers between devices  284 us (20%)
  blocking collectives  249 us (17%)
  matrix products  167 us (12%)
    scatter-add x27, other arithmetic, back_step(): running.at[:, source_row].add(contrib.reshape(full_ch, blocks, BLOCK))  271 us
    gather x54, local copies, waits for them, and re-layouts, back_step(): gathered = extended[:, source_row].reshape(full_ch, row_count)  198 us
    gather x54, local copies, waits for them, and re-layouts, conv_step(): gathered = extended[:, source_row].reshape(full_ch, row_count)  198 us
    psum x1, waiting for transfers between devices, per_device(): weight_grad = lax.psum(kernel_terms, 'box')  174 us
    psum x1, blocking collectives, per_device(): lax.psum((jnp.sum(relu_grad, axis=1), jnp.sum(relu_grad * normed, axis=1)...  125 us
    psum x1, blocking collectives, per_device(): lax.psum((jnp.sum(occupancy * conv, axis=1), jnp.sum(occupancy * conv * c...  123 us
    dot_general x27, matrix products, back_step(): lax.dot_general(kernel_slab, conv_grad, (((0,), (0,)), ((), ())), preferr...  94.8 us
    reduce_scatter x1, waiting for transfers between devices, per_device(): reduced = lax.psum_scatter(ext_grad, 'ch', scatter_dimension=0, tiled=True)  59 us
  transfers between devices with their start and end apart: 7, of which 6 were waited for; matrix products, arithmetic and copies ran while one was open for 1% of the time, Pallas kernels for 0%

commit v1 on v0

v1 whole, which is shorter than its diff:
```python
import functools

import jax
import jax.numpy as jnp
from jax import lax
from jax.experimental import pallas as pl
from jax.experimental.pallas import tpu as pltpu
from jax.sharding import PartitionSpec as P

F32 = jnp.float32
BF16 = jnp.bfloat16
MESH = pl.DeviceIdType.MESH
VMEM = pl.BlockSpec(memory_space=pltpu.VMEM)
SMEM = pl.BlockSpec(memory_space=pltpu.SMEM)
VMEM_LIMIT = 56 * 2**20

BLOCK = 128
BLOCKS = 32
HALF = 16
SLOTS = 8
EXT = BLOCKS + 2 * SLOTS
OFFSETS = 27
CH = 256
LOC = 64
KCH = 9
CHUNKS = OFFSETS // KCH
CROWS = KCH * LOC
WPAD = 1792
NBOX = 64
NA = 4


def params(cid=None):
    if cid is None:
        return pltpu.CompilerParams(vmem_limit_bytes=VMEM_LIMIT)
    return pltpu.CompilerParams(
        vmem_limit_bytes=VMEM_LIMIT, collective_id=cid, has_side_effects=True
    )


def rcopy(src, dst, ssem, rsem, dev):
    return pltpu.make_async_remote_copy(
        src_ref=src, dst_ref=dst, send_sem=ssem, recv_sem=rsem, device_id=dev, device_id_type=MESH
    )


def greet(devs):
    barrier = pltpu.get_barrier_semaphore()
    for dev in devs:
        pl.semaphore_signal(barrier, inc=1, device_id=dev, device_id_type=MESH)
    pl.semaphore_wait(barrier, len(devs))


def rows_of(q):
    return pl.ds(pl.multiple_of(q * LOC, LOC), LOC)


class YGather:
    def __init__(self, own, from_dn, from_up, opp, ssem, rsem):
        q = lax.axis_index("ch")
        self.up = {"ch": lax.rem(q + 1, 4)}
        self.dn = {"ch": lax.rem(q + 3, 4)}
        lo, hi = pl.ds(0, HALF), pl.ds(HALF, HALF)
        mk = lambda src, dst, half, i, dev: rcopy(src.at[half], dst.at[half], ssem.at[i], rsem.at[i], dev)
        self.c = [
            mk(own, from_dn, lo, 0, self.up),
            mk(own, from_up, hi, 1, self.dn),
            mk(own, from_dn, hi, 2, self.up),
            mk(own, from_up, lo, 3, self.dn),
            mk(from_dn, opp, lo, 4, self.up),
            mk(from_up, opp, hi, 5, self.dn),
        ]

    def start(self):
        for i in range(4):
            self.c[i].start()

    def forward(self):
        self.c[0].wait_recv()
        self.c[4].start()
        self.c[1].wait_recv()
        self.c[5].start()

    def wait_near(self):
        self.c[2].wait_recv()
        self.c[3].wait_recv()

    def wait_far(self):
        self.c[4].wait_recv()
        self.c[5].wait_recv()

    def wait_sends(self):
        for c in self.c:
            c.wait_send()


def ext_kernel(
    send_ref, feat_ref, occ_ref, ext_ref, own, from_dn, from_up, opp, fout, fin, ysend, yrecv, fsend, frecv
):
    q = lax.axis_index("ch")
    b = lax.axis_index("box")
    above = {"box": lax.rem(b + 1, NBOX)}
    below = {"box": lax.rem(b + NBOX - 1, NBOX)}
    gather = YGather(own, from_dn, from_up, opp, ysend, yrecv)

    def mask(e, _):
        x = feat_ref[:, pl.ds(pl.multiple_of(e * BLOCK, BLOCK), BLOCK)].astype(F32)
        own[e] = (x * occ_ref[e]).astype(BF16)
        return 0

    lax.fori_loop(0, BLOCKS, mask, 0)
    greet([gather.up, gather.dn, above, below])
    gather.start()

    def pack(r, src):
        for d in range(2):
            for s in range(SLOTS):
                pick = send_ref[d * SLOTS + s]
                blk = src[jnp.minimum(pick, BLOCKS - 1)].astype(F32)
                fout[r, d, s] = jnp.where(pick < BLOCKS, blk, 0.0).astype(BF16)
        up = rcopy(fout.at[r, 1], fin.at[r, 0], fsend.at[r, 1], frecv.at[r, 0], above)
        dn = rcopy(fout.at[r, 0], fin.at[r, 1], fsend.at[r, 0], frecv.at[r, 1], below)
        up.start()
        dn.start()
        return up, dn

    def place(r_abs, src):
        rows = rows_of(r_abs)

        def one(e, _):
            ext_ref[e, rows, :] = src[e]
            return 0

        lax.fori_loop(0, BLOCKS, one, 0)

    q_dn, q_up, q_opp = lax.rem(q + 3, 4), lax.rem(q + 1, 4), lax.rem(q + 2, 4)
    copies = [pack(0, own)]
    place(q, own)
    ext_ref[EXT] = jnp.zeros((CH, BLOCK), BF16)
    gather.forward()
    gather.wait_near()
    copies.append(pack(1, from_dn))
    copies.append(pack(2, from_up))
    place(q_dn, from_dn)
    place(q_up, from_up)
    gather.wait_far()
    copies.append(pack(3, opp))
    place(q_opp, opp)
    keep_below = jnp.where(b > 0, 1.0, 0.0)
    keep_above = jnp.where(b < NBOX - 1, 1.0, 0.0)
    for r, r_abs in enumerate((q, q_dn, q_up, q_opp)):
        up, dn = copies[r]
        up.wait_recv()
        dn.wait_recv()
        rows = rows_of(r_abs)
        for s in range(SLOTS):
            ext_ref[BLOCKS + s, rows, :] = (fin[r, 0, s].astype(F32) * keep_below).astype(BF16)
            ext_ref[BLOCKS + SLOTS + s, rows, :] = (fin[r, 1, s].astype(F32) * keep_above).astype(BF16)
    gather.wait_sends()
    for up, dn in copies:
        up.wait_send()
        dn.wait_send()


def make_ext(send, features, occ):
    quarter = pltpu.VMEM((BLOCKS, LOC, BLOCK), BF16)
    return pl.pallas_call(
        ext_kernel,
        out_shape=jax.ShapeDtypeStruct((EXT + 1, CH, BLOCK), BF16),
        in_specs=[SMEM, VMEM, VMEM],
        out_specs=VMEM,
        scratch_shapes=[
            quarter,
            quarter,
            quarter,
            quarter,
            pltpu.VMEM((4, 2, SLOTS, LOC, BLOCK), BF16),
            pltpu.VMEM((4, 2, SLOTS, LOC, BLOCK), BF16),
            pltpu.SemaphoreType.DMA((6,)),
            pltpu.SemaphoreType.DMA((6,)),
            pltpu.SemaphoreType.DMA((4, 2)),
            pltpu.SemaphoreType.DMA((4, 2)),
        ],
        compiler_params=params(1),
        name="extend",
    )(send, features, occ)


def conv_kernel(map_ref, w_ref, ext_ref, occ_ref, conv_ref, sum_ref, p_ref):
    p_ref[EXT] = jnp.zeros((CROWS, BLOCK), F32)
    for c in range(CHUNKS):

        def tile(t, _):
            rhs = jnp.concatenate([ext_ref[2 * t], ext_ref[2 * t + 1]], axis=1)
            res = jnp.dot(w_ref[pl.ds(c * CROWS, CROWS), :], rhs, preferred_element_type=F32)
            p_ref[2 * t] = res[:, :BLOCK]
            p_ref[2 * t + 1] = res[:, BLOCK:]
            return 0

        lax.fori_loop(0, EXT // 2, tile, 0)

        def out(j, _):
            acc = None
            for k in range(KCH):
                v = p_ref[map_ref[(c * KCH + k) * BLOCKS + j], pl.ds(LOC * k, LOC), :]
                acc = v if acc is None else acc + v
            if c == 0:
                conv_ref[j] = acc
            else:
                conv_ref[j] += acc
            return 0

        lax.fori_loop(0, BLOCKS, out, 0)

    def stats(j, carry):
        a, b = carry
        x = conv_ref[j]
        o = occ_ref[j] * x
        return a + o, b + o * x

    zero = jnp.zeros((LOC, BLOCK), F32)
    a, b = lax.fori_loop(0, BLOCKS, stats, (zero, zero))
    sum_ref[0] = a
    sum_ref[1] = b


def conv_call(kmap, w, ext, occ):
    return pl.pallas_call(
        conv_kernel,
        out_shape=(
            jax.ShapeDtypeStruct((BLOCKS, LOC, BLOCK), F32),
            jax.ShapeDtypeStruct((2, LOC, BLOCK), F32),
        ),
        in_specs=[SMEM, VMEM, VMEM, VMEM],
        out_specs=(VMEM, VMEM),
        scratch_shapes=[pltpu.VMEM((EXT + 1, CROWS, BLOCK), F32)],
        compiler_params=params(),
        name="conv",
    )(kmap, w, ext, occ)


def lane_masks():
    ch = lax.broadcasted_iota(jnp.int32, (LOC, BLOCK), 0)
    lane = lax.broadcasted_iota(jnp.int32, (LOC, BLOCK), 1)
    return lane == ch, lane == ch + LOC


def to_row(first, second):
    m0, m1 = lane_masks()
    c0 = jnp.sum(first, axis=1, keepdims=True)
    c1 = jnp.sum(second, axis=1, keepdims=True)
    return jnp.sum(jnp.where(m0, c0, 0.0) + jnp.where(m1, c1, 0.0), axis=0, keepdims=True)


def to_cols(row):
    m0, m1 = lane_masks()
    return (
        jnp.sum(jnp.where(m0, row, 0.0), axis=1, keepdims=True),
        jnp.sum(jnp.where(m1, row, 0.0), axis=1, keepdims=True),
    )


def box_groups():
    b = lax.axis_index("box")
    hi, lo = b // 8, lax.rem(b, 8)
    near = [{"box": hi * 8 + lax.rem(lo + d, 8)} for d in range(1, 8)]
    far = [{"box": lax.rem(hi + d, 8) * 8 + lo} for d in range(1, 8)]
    return (lo, near), (hi, far)


def box_sum(mine, buf, ssem, rsem):
    for step, (me, peers) in enumerate(box_groups()):
        buf[step, me] = mine
        copies = []
        for d, dev in enumerate(peers):
            c = rcopy(buf.at[step, me], buf.at[step, me], ssem.at[step, d], rsem.at[step, d], dev)
            c.start()
            copies.append(c)
        for c in copies:
            c.wait_recv()
        mine = buf[step, 0]
        for d in range(1, 8):
            mine = mine + buf[step, d]
        for c in copies:
            c.wait_send()
    return mine


def norm_kernel(
    map_ref,
    conv_ref,
    sum_ref,
    grad_ref,
    occ_ref,
    gs_ref,
    ext_ref,
    out_ref,
    cga_ref,
    wg_ref,
    stat_ref,
    normed,
    rgrad,
    own,
    from_dn,
    from_up,
    opp,
    sbuf,
    ysend,
    yrecv,
    ssend,
    srecv,
):
    q = lax.axis_index("ch")
    gather = YGather(own, from_dn, from_up, opp, ysend, yrecv)
    (_, near), (_, far) = box_groups()
    sub = lax.broadcasted_iota(jnp.int32, (8, BLOCK), 0)
    count = jnp.sum(occ_ref[...], axis=0)
    count = jnp.broadcast_to(jnp.sum(count, axis=1, keepdims=True), (1, BLOCK))
    row = to_row(sum_ref[0], sum_ref[1])
    pay = jnp.where(sub == 0, row, jnp.where(sub == 1, count, 0.0))
    greet([gather.up, gather.dn] + near + far)
    tot = box_sum(pay, sbuf.at[0], ssend.at[0], srecv.at[0])
    n_vox = tot[1:2, 0:1]
    s1, s2 = to_cols(tot[0:1, :])
    mean = s1 / n_vox
    var = s2 / n_vox - mean * mean
    inv = 1.0 / jnp.sqrt(var + 1e-05)
    gain, shift = to_cols(gs_ref[...])

    def fwd(j, carry):
        a, b = carry
        cols = pl.ds(pl.multiple_of(j * BLOCK, BLOCK), BLOCK)
        occ = occ_ref[j]
        nd = (conv_ref[j] - mean) * inv
        sh = nd * gain + shift
        out_ref[:, cols] = (occ * jnp.maximum(sh, 0.0)).astype(BF16)
        rg = jnp.where(sh > 0.0, occ * grad_ref[:, cols].astype(F32), 0.0)
        normed[j] = nd
        rgrad[j] = rg
        return a + rg, b + rg * nd

    zero = jnp.zeros((LOC, BLOCK), F32)
    a, b = lax.fori_loop(0, BLOCKS, fwd, (zero, zero))
    row = to_row(a, b)
    tot = box_sum(jnp.where(sub == 0, row, 0.0), sbuf.at[1], ssend.at[1], srecv.at[1])
    stat_ref[...] = tot[0:1, :]
    sg, gg = to_cols(tot[0:1, :])
    scale = inv * gain
    sgm = sg / n_vox

    def bwd(j, _):
        nd = normed[j]
        own[j] = (occ_ref[j] * scale * (rgrad[j] - sgm - nd * gg / n_vox)).astype(BF16)
        return 0

    lax.fori_loop(0, BLOCKS, bwd, 0)
    gather.start()
    gather.forward()

    def kterm(k, _):
        acc = jnp.zeros((LOC, CH), F32)
        for t in range(BLOCKS // 2):
            lhs = jnp.concatenate([own[2 * t], own[2 * t + 1]], axis=1)
            rhs = jnp.concatenate(
                [ext_ref[map_ref[k * BLOCKS + 2 * t]], ext_ref[map_ref[k * BLOCKS + 2 * t + 1]]], axis=1
            )
            acc += lax.dot_general(lhs, rhs, (((1,), (1,)), ((), ())), preferred_element_type=F32)
        wg_ref[k] = acc
        return 0

    lax.fori_loop(0, OFFSETS, kterm, 0)

    def place(r_abs, src):
        rows = rows_of(r_abs)

        def one(e, _):
            cga_ref[e, rows, :] = src[e]
            return 0

        lax.fori_loop(0, BLOCKS, one, 0)

    place(q, own)
    gather.wait_near()
    place(lax.rem(q + 3, 4), from_dn)
    place(lax.rem(q + 1, 4), from_up)
    gather.wait_far()
    place(lax.rem(q + 2, 4), opp)
    gather.wait_sends()


def norm_call(kmap, conv, sums, out_grad, occ, gs, ext):
    quarter = pltpu.VMEM((BLOCKS, LOC, BLOCK), BF16)
    return pl.pallas_call(
        norm_kernel,
        out_shape=(
            jax.ShapeDtypeStruct((LOC, BLOCKS * BLOCK), BF16),
            jax.ShapeDtypeStruct((BLOCKS, CH, BLOCK), BF16),
            jax.ShapeDtypeStruct((OFFSETS, LOC, CH), F32),
            jax.ShapeDtypeStruct((1, BLOCK), F32),
        ),
        in_specs=[SMEM] + [VMEM] * 6,
        out_specs=(VMEM,) * 4,
        scratch_shapes=[
            pltpu.VMEM((BLOCKS, LOC, BLOCK), F32),
            pltpu.VMEM((BLOCKS, LOC, BLOCK), F32),
            quarter,
            quarter,
            quarter,
            quarter,
            pltpu.VMEM((2, 2, 8, 8, BLOCK), F32),
            pltpu.SemaphoreType.DMA((6,)),
            pltpu.SemaphoreType.DMA((6,)),
            pltpu.SemaphoreType.DMA((2, 2, 7)),
            pltpu.SemaphoreType.DMA((2, 2, 7)),
        ],
        compiler_params=params(2),
        name="norm",
    )(kmap, conv, sums, out_grad, occ, gs, ext)


def back_kernel(map_ref, w_ref, cg_ref, eg_ref, q_ref, *accs):
    for a in accs:

        def zero(e, _):
            a[e] = jnp.zeros((LOC, BLOCK), F32)
            return 0

        lax.fori_loop(0, EXT + 1, zero, 0)
    for c in range(CHUNKS):

        def tile(t, _):
            rhs = jnp.concatenate([cg_ref[2 * t], cg_ref[2 * t + 1]], axis=1)
            res = jnp.dot(w_ref[pl.ds(c * CROWS, CROWS), :], rhs, preferred_element_type=F32)
            q_ref[2 * t] = res[:, :BLOCK]
            q_ref[2 * t + 1] = res[:, BLOCK:]
            return 0

        lax.fori_loop(0, BLOCKS // 2, tile, 0)

        def scatter(t, _):
            for k in range(KCH):
                for i in range(NA):
                    j = t * NA + i
                    m = map_ref[(c * KCH + k) * BLOCKS + j]
                    accs[i][m] = accs[i][m] + q_ref[j, pl.ds(LOC * k, LOC), :]
            return 0

        lax.fori_loop(0, BLOCKS // NA, scatter, 0)

    def finish(e, _):
        s = accs[0][e]
        for a in accs[1:]:
            s = s + a[e]
        eg_ref[e] = s
        return 0

    lax.fori_loop(0, EXT, finish, 0)


def back_call(kmap, w, cga):
    return pl.pallas_call(
        back_kernel,
        out_shape=jax.ShapeDtypeStruct((EXT, LOC, BLOCK), F32),
        in_specs=[SMEM, VMEM, VMEM],
        out_specs=VMEM,
        scratch_shapes=[pltpu.VMEM((BLOCKS, CROWS, BLOCK), F32)]
        + [pltpu.VMEM((EXT + 1, LOC, BLOCK), F32)] * NA,
        compiler_params=params(),
        name="back",
    )(kmap, w, cga)


def final_kernel(
    send_ref, eg_ref, occ_ref, wg_ref, in_ref, wout_ref, fout, fin, half, halfin, zbuf, zin, red, xin, res, fsend, frecv, csend, crecv, zsend, zrecv, xsend, xrecv, asend, arecv, esend, erecv
):
    b = lax.axis_index("box")
    core = lax.rem(b, 2)
    z = lax.rem(b // 2, 8)
    x = b // 16
    dev = lambda xx, zz, cc: {"box": xx * 16 + zz * 2 + cc}
    above = {"box": lax.rem(b + 1, NBOX)}
    below = {"box": lax.rem(b + NBOX - 1, NBOX)}
    mate = dev(x, z, 1 - core)
    zpeers = [dev(x, lax.rem(z + d, 8), core) for d in range(1, 8)]
    xpeers = [dev(lax.rem(x + d, 4), z, core) for d in range(1, 4)]
    KP = 28

    def cut(k, _):
        lo, hi = wg_ref[k, :, :BLOCK], wg_ref[k, :, BLOCK:]
        keep = jnp.where(core == 0, lo, hi)
        give = jnp.where(core == 0, hi, lo)
        half[k] = give.astype(BF16)
        red[k] = keep
        return 0

    lax.fori_loop(0, OFFSETS, cut, 0)
    half[OFFSETS] = jnp.zeros((LOC, BLOCK), BF16)
    red[OFFSETS] = jnp.zeros((LOC, BLOCK), F32)
    for s in range(SLOTS):
        fout[0, s] = eg_ref[BLOCKS + s].astype(BF16)
        fout[1, s] = eg_ref[BLOCKS + SLOTS + s].astype(BF16)
    greet([above, below, mate] + zpeers + xpeers)
    cm = rcopy(half, halfin, csend, crecv, mate)
    cm.start()
    f0 = rcopy(fout.at[0], fin.at[0], fsend.at[0], frecv.at[0], below)
    f1 = rcopy(fout.at[1], fin.at[1], fsend.at[1], frecv.at[1], above)
    f0.start()
    f1.start()
    cm.wait_recv()
    rows = KP * LOC // 8

    def add(k, _):
        t = red[k] + halfin[k].astype(F32)
        red[k] = t
        zbuf[pl.ds(pl.multiple_of(k * LOC, LOC), LOC), :] = t.astype(BF16)
        return 0

    lax.fori_loop(0, KP, add, 0)
    part = lambda zz: pl.ds(pl.multiple_of(zz * rows, 16), rows)
    zc = []
    for d in range(1, 8):
        c = rcopy(zbuf.at[part(lax.rem(z + d, 8))], zin.at[d - 1], zsend.at[d - 1], zrecv.at[d - 1], zpeers[d - 1])
        c.start()
        zc.append(c)

    f0.wait_recv()
    f1.wait_recv()
    up_ok = b < NBOX - 1
    dn_ok = b > 0

    def settle(d, _):
        t = eg_ref[d]
        for s in range(SLOTS):
            t = t + jnp.where((send_ref[SLOTS + s] == d) & up_ok, fin[0, s].astype(F32), 0.0)
            t = t + jnp.where((send_ref[s] == d) & dn_ok, fin[1, s].astype(F32), 0.0)
        in_ref[:, pl.ds(pl.multiple_of(d * BLOCK, BLOCK), BLOCK)] = (occ_ref[d] * t).astype(BF16)
        return 0

    lax.fori_loop(0, BLOCKS, settle, 0)

    for c in zc:
        c.wait_recv()
    tot = zbuf[part(z), :].astype(F32)
    for d in range(7):
        tot = tot + zin[d].astype(F32)
    xin[x] = tot.astype(BF16)
    xc = []
    for d in range(1, 4):
        c = rcopy(xin.at[x], xin.at[x], xsend.at[d - 1], xrecv.at[d - 1], xpeers[d - 1])
        c.start()
        xc.append(c)
    for c in xc:
        c.wait_recv()
    tot = xin[0].astype(F32)
    for d in range(1, 4):
        tot = tot + xin[d].astype(F32)
    for c in xc:
        c.wait_send()
    for c in zc:
        c.wait_send()
    res[0, part(z), :] = tot.astype(BF16)
    ac = []
    for d in range(1, 8):
        c = rcopy(res.at[0, part(z)], res.at[0, part(z)], asend.at[d - 1], arecv.at[d - 1], zpeers[d - 1])
        c.start()
        ac.append(c)
    for d in range(1, 8):
        src = lax.rem(z + 8 - d, 8)
        rcopy(res.at[0, part(src)], res.at[0, part(src)], asend.at[d - 1], arecv.at[d - 1], zpeers[d - 1]).wait_recv()
    e = rcopy(res.at[0], res.at[1], esend, erecv, mate)
    e.start()
    e.wait_recv()

    def put(k, _):
        r = pl.ds(pl.multiple_of(k * LOC, LOC), LOC)
        m = res[0, r, :].astype(F32)
        o = res[1, r, :].astype(F32)
        wout_ref[k, :, :BLOCK] = jnp.where(core == 0, m, o)
        wout_ref[k, :, BLOCK:] = jnp.where(core == 0, o, m)
        return 0

    lax.fori_loop(0, OFFSETS, put, 0)
    e.wait_send()
    for c in ac:
        c.wait_send()
    cm.wait_send()
    f0.wait_send()
    f1.wait_send()


def final_call(send, eg, occ, wg):
    KP = 28
    rows = KP * LOC // 8
    dma = pltpu.SemaphoreType.DMA
    return pl.pallas_call(
        final_kernel,
        out_shape=(
            jax.ShapeDtypeStruct((LOC, BLOCKS * BLOCK), BF16),
            jax.ShapeDtypeStruct((OFFSETS, LOC, CH), F32),
        ),
        in_specs=[SMEM, VMEM, VMEM, VMEM],
        out_specs=(VMEM, VMEM),
        scratch_shapes=[
            pltpu.VMEM((2, SLOTS, LOC, BLOCK), BF16),
            pltpu.VMEM((2, SLOTS, LOC, BLOCK), BF16),
            pltpu.VMEM((KP, LOC, BLOCK), BF16),
            pltpu.VMEM((KP, LOC, BLOCK), BF16),
            pltpu.VMEM((KP * LOC, BLOCK), BF16),
            pltpu.VMEM((7, rows, BLOCK), BF16),
            pltpu.VMEM((KP, LOC, BLOCK), F32),
            pltpu.VMEM((4, rows, BLOCK), BF16),
            pltpu.VMEM((2, KP * LOC, BLOCK), BF16),
            dma((2,)),
            dma((2,)),
            dma,
            dma,
            dma((7,)),
            dma((7,)),
            dma((3,)),
            dma((3,)),
            dma((7,)),
            dma((7,)),
            dma,
            dma,
        ],
        compiler_params=params(3),
        name="final",
    )(send, eg, occ, wg)


def per_device(
    features, occupied, send_lists, kernel_map, weights, norm_gain, norm_shift, out_grad
):
    occ = occupied.astype(F32).reshape(BLOCKS, 1, BLOCK)
    send = send_lists.reshape(2 * SLOTS)
    kmap = kernel_map.reshape(OFFSETS * BLOCKS)
    w = weights.reshape(OFFSETS * LOC, CH)
    gs = jnp.concatenate([norm_gain, norm_shift]).reshape(1, BLOCK)
    parts = weights.reshape(OFFSETS, LOC, 4, LOC).transpose(2, 0, 3, 1)
    whole = lax.all_to_all(parts, "ch", split_axis=0, concat_axis=0)
    w_in = whole.transpose(1, 2, 0, 3).reshape(OFFSETS * LOC, CH)

    ext = make_ext(send, features, occ)
    conv, sums = conv_call(kmap, w, ext, occ)
    out_features, cga, wg, stat = norm_call(kmap, conv, sums, out_grad, occ, gs, ext)
    eg = back_call(kmap, w_in, cga)
    in_grad, weight_grad = final_call(send, eg, occ, wg)
    return (out_features, in_grad, weight_grad, stat[0, LOC:], stat[0, :LOC])


def solution(mesh):
    in_specs = (
        P("ch", "box"),
        P("box"),
        P("box", None, None),
        P("box", None, None),
        P(None, "ch", None),
        P("ch"),
        P("ch"),
        P("ch", "box"),
    )
    out_specs = (P("ch", "box"), P("ch", "box"), P(None, "ch", None), P("ch"), P("ch"))
    return jax.shard_map(
        per_device, mesh=mesh, in_specs=in_specs, out_specs=out_specs, check_vma=False
    )
```

time: 1430 us -> 211 us (0.15)
  local copies, waits for them, and re-layouts: 409 us -> 19 us
  other arithmetic: 286 us -> 1.23 us
  waiting for transfers between devices: 284 us -> 0.01 us
  blocking collectives: 249 us -> 0 us
  Pallas kernels: 0 us -> 185 us
  matrix products: 167 us -> 0 us
    gather x110 -> x0, local copies, waits for them, and re-layouts: 401 us -> none  [the longest x54 198 us: back_step(): gathered = extended[:, source_row].reshape(full_ch, row_count)]
    scatter-add x29 -> x0, other arithmetic: 273 us -> none  [the longest x27 271 us: back_step(): running.at[:, source_row].add(contrib.reshape(full_ch, blocks, BLOCK))]
    psum x2 -> x0, blocking collectives: 249 us -> none  [the longest x1 125 us: per_device(): lax.psum((jnp.sum(relu_grad, axis=1), jnp.sum(relu_grad * normed, axis=1)...]
    pallas_call x0 -> x5, Pallas kernels: none -> 185 us  [the longest x1 64.1 us: norm_call(): pl.pallas_call(norm_kernel, out_shape=(jax.ShapeDtypeStruct((LOC, BLOCKS...]
    psum x1 -> x0, waiting for transfers between devices: 174 us -> none  [per_device(): weight_grad = lax.psum(kernel_terms, 'box')]
    dot_general x81 -> x0, matrix products: 167 us -> none  [the longest x27 94.8 us: back_step(): lax.dot_general(kernel_slab, conv_grad, (((0,), (0,)), ((), ())), preferr...]
    reduce_scatter x1 -> x0, waiting for transfers between devices: 59 us -> none  [per_device(): reduced = lax.psum_scatter(ext_grad, 'ch', scatter_dimension=0, tiled=True)]
    all_gather x1 -> x0, waiting for transfers between devices: 38 us -> none  [per_device(): whole = lax.all_gather(padded_local, 'ch', axis=0, tiled=True)]
  transfers between devices with their start and end apart: 7 -> 1, of which waited for: 6 -> 0; matrix products, arithmetic and copies ran while one was open for 1% -> 2% of each run, Pallas kernels for 0% -> 58%
where the time goes in v1:
time: 211 us
  Pallas kernels  185 us (88%)
  local copies, waits for them, and re-layouts  19 us (9%)
  starting transfers between devices  5.01 us (2%)
    pallas_call x1, Pallas kernels, norm_call(): pl.pallas_call(norm_kernel, out_shape=(jax.ShapeDtypeStruct((LOC, BLOCKS...  64.1 us
    pallas_call x1, Pallas kernels, final_call(): pl.pallas_call(final_kernel, out_shape=(jax.ShapeDtypeStruct((LOC, BLOCKS...  42.8 us
    pallas_call x1, Pallas kernels, make_ext(): pl.pallas_call(ext_kernel, out_shape=jax.ShapeDtypeStruct((EXT + 1, CH, B...  35.4 us
    pallas_call x1, Pallas kernels, conv_call(): pl.pallas_call(conv_kernel, out_shape=(jax.ShapeDtypeStruct((BLOCKS, LOC,...  23.1 us
    pallas_call x1, Pallas kernels, back_call(): pl.pallas_call(back_kernel, out_shape=jax.ShapeDtypeStruct((EXT, LOC, BLO...  19.2 us
    unnamed x19, local copies, waits for them, and re-layouts  7.73 us
    all_to_all x1, starting transfers between devices, per_device(): whole = lax.all_to_all(parts, 'ch', split_axis=0, concat_axis=0)  5.01 us
  transfers between devices with their start and end apart: 1, of which 0 were waited for; matrix products, arithmetic and copies ran while one was open for 2% of the time, Pallas kernels for 58%

profile of v1, /device:TPU:1, one launch (start us, length us, event | category | flops | bytes accessed | tf_op | source)
XLA Modules:
  0.0 210.5 jit_solution(6803374769793171095)
XLA Ops:
  0.6 3.0 %reshape.36 = bf16[27,64,4,64]{3,2,1,0:T(4,128)(2,1)S(1)} reshape(bf16[27,64,256]{2,1,0:T(8,128)(2,1)} %param.12) | data formatting | bytes 1769472 | tf_op jit(solution)/shard_map/reshape | solution.py:639
  3.6 2.3 %copy.15 = bf16[4,27,64,64]{3,2,1,0:T(8,128)(2,1)S(1)} copy(bf16[4,27,64,64]{2,0,3,1:T(4,128)(2,1)S(1)} %bitcast.11) | data formatting | bytes 1769472 | tf_op jit(solution)/shard_map/transpose | solution.py:639
  5.9 0.0 copy-start.2
  5.9 0.0 copy-start.4
  6.0 0.0 copy-start.3
  6.0 2.5 %reshape.39 = bf16[4,2,55296]{2,1,0:T(2,128)(2,1)} reshape(bf16[4,27,64,64]{3,2,1,0:T(8,128)(2,1)S(1)} %copy.15) | data formatting | bytes 1769472
  8.5 5.0 %all-to-all-start = ((bf16[4,2,55296]{2,1,0:T(2,128)(2,1)}), bf16[4,2,55296]{2,1,0:T(2,128)(2,1)S(1)}, u32[]{:S(2)}, u32[]{:S(2)}) async-start(bf16[4,2,55296]{2,1,0:T(2,128)(2,1)} %reshape.39), calls=%async_computation | async-start | bytes 1769472 | tf_op jit(solution)/shard_map/all_to_all | solution.py:640
  13.5 0.0 copy-done.2
  13.5 0.6 convert_element_type.3
  14.1 0.0 copy-done.4
  14.1 0.6 reshape.33.send_ref
  14.7 0.0 copy-done.3
  14.8 0.7 reshape.31.map_ref
  15.4 35.4 %extend.1.ext_ref = bf16[49,256,128]{2,1,0:T(8,128)(2,1)} custom-call(s32[16]{0:T(128)} %reshape.33.send_ref, bf16[64,4096]{1,0:T(8,128)(2,1)} %feat_ref.1, f32[32,1,128]{2,1,0:T(1,128)} %bitcast.13), custom_call_target="tpu_custom_call" | custom-call | tf_op jit(solution)/shard_map/extend/pallas_call | solution.py:167
  50.8 0.0 copy-start.5
  50.8 0.0 copy-start.6
  50.8 23.1 %conv.1 = (f32[32,64,128]{2,1,0:T(8,128)}, f32[2,64,128]{2,1,0:T(8,128)}) custom-call(s32[864]{0:T(1024)} %reshape.31.map_ref, bf16[1728,256]{1,0:T(8,128)(2,1)} %bitcast.12, bf16[49,256,128]{2,1,0:T(8,128)(2,1)} %extend.1.ext_ref, f32[32,1,128]{2,1,0:T(1,128)} %bitcast.14), custom_call_target="tpu_custom_call" | custom-call | tf_op jit(solution)/shard_map/conv/pallas_call | solution.py:228
  73.9 0.0 copy-done.5
  73.9 0.0 copy-done.6
  73.9 0.6 maximum_bitcast_fusion.gs_ref
  74.5 64.1 %norm.1 = (bf16[64,4096]{1,0:T(8,128)(2,1)}, bf16[32,256,128]{2,1,0:T(8,128)(2,1)}, f32[27,64,256]{2,1,0:T(8,128)}, f32[1,128]{1,0:T(1,128)}) custom-call(s32[864]{0:T(1024)} %reshape.31.map_ref, f32[32,64,128]{2,1,0:T(8,128)} %get-tuple-element.13.conv_ref, f32[2,64,128]{2,1,0:T(8,128)} %get-tuple-element.14.sum_ref, bf16[64,4096]{1,0:T(8,128)(2,1)} %grad_ref.1, ...), custom_call_target="tpu_custom_call" | custom-call | tf_op jit(solution)/shard_map/norm/pallas_call | solution.py:393
  138.7 1.2 slice_bitcast_fusion
  139.9 0.0 all-to-all-done
  139.9 1.3 reshape.40
  141.2 1.6 copy.16
  142.8 1.9 reshape.37.w_ref
  144.7 19.2 %back.1.eg_ref = f32[48,64,128]{2,1,0:T(8,128)} custom-call(s32[864]{0:T(1024)} %reshape.31.map_ref, bf16[1728,256]{1,0:T(8,128)(2,1)} %reshape.37.w_ref, bf16[32,256,128]{2,1,0:T(8,128)(2,1)} %get-tuple-element.16.cg_ref), custom_call_target="tpu_custom_call" | custom-call | tf_op jit(solution)/shard_map/back/pallas_call | solution.py:461
  163.9 0.0 copy-start.1
  163.9 42.8 %final.1 = (bf16[64,4096]{1,0:T(8,128)(2,1)}, f32[27,64,256]{2,1,0:T(8,128)}) custom-call(s32[16]{0:T(128)} %reshape.33.send_ref, f32[48,64,128]{2,1,0:T(8,128)} %back.1.eg_ref, f32[32,1,128]{2,1,0:T(1,128)} %bitcast.16, f32[27,64,256]{2,1,0:T(8,128)} %get-tuple-element.17.wg_ref), custom_call_target="tpu_custom_call" | custom-call | tf_op jit(solution)/shard_map/final/pallas_call | solution.py:595
  206.7 0.0 copy-start
  206.7 0.0 copy-done.1
  206.7 0.8 copy.20
  207.5 1.9 copy.21
  209.3 0.0 copy-done
  209.3 1.2 copy.22
  (1 shorter events, 0.0 us)
Async XLA Ops:
  5.9 7.6 %copy-start.2 = (s32[4096]{0:T(1024)S(1)}, s32[4096]{0:T(1024)}, u32[]{:S(2)}) copy-start(s32[4096]{0:T(1024)} %param.9) | copy-start | bytes 49156
  5.9 8.2 %copy-start.4 = (s32[1,2,8]{2,1,0:T(2,128)S(1)}, s32[1,2,8]{2,1,0:T(2,128)}, u32[]{:S(2)}) copy-start(s32[1,2,8]{2,1,0:T(2,128)} %param.10) | copy-start | bytes 196
  6.0 8.8 %copy-start.3 = (s32[1,27,32]{2,0,1:T(1,128)S(1)}, s32[1,27,32]{2,0,1:T(1,128)}, u32[]{:S(2)}) copy-start(s32[1,27,32]{2,0,1:T(1,128)} %param.11) | copy-start | bytes 10372
  8.5 131.4 %all-to-all-start = ((bf16[4,2,55296]{2,1,0:T(2,128)(2,1)}), bf16[4,2,55296]{2,1,0:T(2,128)(2,1)S(1)}, u32[]{:S(2)}, u32[]{:S(2)}) async-start(bf16[4,2,55296]{2,1,0:T(2,128)(2,1)} %reshape.39), calls=%async_computation | async-start | bytes 1769472 | tf_op jit(solution)/shard_map/all_to_all | solution.py:640
  50.8 23.1 %copy-start.5 = (f32[64]{0:T(128)S(1)}, f32[64]{0:T(128)}, u32[]{:S(2)}) copy-start(f32[64]{0:T(128)} %param.14) | copy-start | bytes 772
  50.8 23.1 %copy-start.6 = (f32[64]{0:T(128)S(1)}, f32[64]{0:T(128)}, u32[]{:S(2)}) copy-start(f32[64]{0:T(128)} %param.13) | copy-start | bytes 772
  163.9 42.8 %copy-start.1 = (bf16[64,4096]{1,0:T(8,128)(2,1)S(1)}, bf16[64,4096]{1,0:T(8,128)(2,1)}, u32[]{:S(2)}) copy-start(bf16[64,4096]{1,0:T(8,128)(2,1)} %get-tuple-element.28) | copy-start | bytes 1572868
  206.7 2.7 %copy-start = (f32[27,64,256]{2,1,0:T(8,128)S(1)}, f32[27,64,256]{2,1,0:T(8,128)}, u32[]{:S(2)}) copy-start(f32[27,64,256]{2,1,0:T(8,128)} %get-tuple-element.30) | copy-start | bytes 5308420

commit v2 on v1

v2 whole, which is shorter than its diff:
```python
import functools

import jax
import jax.numpy as jnp
from jax import lax
from jax.experimental import pallas as pl
from jax.experimental.pallas import tpu as pltpu
from jax.sharding import PartitionSpec as P

F32 = jnp.float32
BF16 = jnp.bfloat16
MESH = pl.DeviceIdType.MESH
VMEM = pl.BlockSpec(memory_space=pltpu.VMEM)
SMEM = pl.BlockSpec(memory_space=pltpu.SMEM)
VMEM_LIMIT = 60 * 2**20

BLOCK = 128
BLOCKS = 32
CHUNK = 8
SLOTS = 8
EXT = BLOCKS + 2 * SLOTS
OFFSETS = 27
CH = 256
LOC = 64
WPAD = 1792
WROWS = 2048
XROWS = WROWS // 4
ZROWS = XROWS // 8
NBOX = 64
NA = 4


def params(cid=None):
    if cid is None:
        return pltpu.CompilerParams(vmem_limit_bytes=VMEM_LIMIT)
    return pltpu.CompilerParams(
        vmem_limit_bytes=VMEM_LIMIT, collective_id=cid, has_side_effects=True
    )


def rcopy(src, dst, ssem, rsem, dev):
    return pltpu.make_async_remote_copy(
        src_ref=src, dst_ref=dst, send_sem=ssem, recv_sem=rsem, device_id=dev, device_id_type=MESH
    )


def greet(devs):
    barrier = pltpu.get_barrier_semaphore()
    for dev in devs:
        pl.semaphore_signal(barrier, inc=1, device_id=dev, device_id_type=MESH)
    pl.semaphore_wait(barrier, len(devs))


def rows_of(q):
    return pl.ds(pl.multiple_of(q * LOC, LOC), LOC)


class YGather:
    def __init__(self, own, from_dn, from_up, opp, ssem, rsem):
        q = lax.axis_index("ch")
        self.up = {"ch": lax.rem(q + 1, 4)}
        self.dn = {"ch": lax.rem(q + 3, 4)}

        def mk(src, dst, chunk, i, dev):
            part = pl.ds(chunk * CHUNK, CHUNK)
            return rcopy(src.at[part], dst.at[part], ssem.at[i], rsem.at[i], dev)

        self.own_up = [mk(own, from_dn, c, c, self.up) for c in range(4)]
        self.own_dn = [mk(own, from_up, c, 4 + c, self.dn) for c in range(4)]
        self.far_up = [mk(from_dn, opp, c, 8 + c, self.up) for c in (0, 1)]
        self.far_dn = [mk(from_up, opp, c, 8 + c, self.dn) for c in (2, 3)]

    def start(self):
        self.own_up[0].start()
        self.own_dn[2].start()
        self.own_up[1].start()
        self.own_dn[3].start()

    def forward(self, i):
        self.own_up[i].wait_recv()
        self.far_up[i].start()
        self.own_up[2 + i].start()
        self.own_dn[2 + i].wait_recv()
        self.far_dn[i].start()
        self.own_dn[i].start()

    def wait_part(self, i):
        self.own_up[2 + i].wait_recv()
        self.own_dn[i].wait_recv()
        self.far_up[i].wait_recv()
        self.far_dn[i].wait_recv()

    def wait_sends(self):
        for c in self.own_up + self.own_dn + self.far_up + self.far_dn:
            c.wait_send()


def conv_kernel(
    send_ref,
    map_ref,
    feat_ref,
    occ_ref,
    w_ref,
    conv_ref,
    sum_ref,
    extt_ref,
    parts_ref,
    own,
    from_dn,
    from_up,
    opp,
    fout,
    fin,
    ext,
    prod,
    ysend,
    yrecv,
    fsend,
    frecv,
):
    q = lax.axis_index("ch")
    b = lax.axis_index("box")
    above = {"box": lax.rem(b + 1, NBOX)}
    below = {"box": lax.rem(b + NBOX - 1, NBOX)}
    gather = YGather(own, from_dn, from_up, opp, ysend, yrecv)
    quarters = ((q, own), (lax.rem(q + 3, 4), from_dn), (lax.rem(q + 1, 4), from_up), (lax.rem(q + 2, 4), opp))

    def mask(e, _):
        x = feat_ref[:, pl.ds(pl.multiple_of(e * BLOCK, BLOCK), BLOCK)].astype(F32)
        own[e] = (x * occ_ref[e]).astype(BF16)
        return 0

    lax.fori_loop(0, BLOCKS, mask, 0)
    greet([gather.up, gather.dn, above, below])
    gather.start()

    def pack(r, src):
        for d in range(2):
            for s in range(SLOTS):
                pick = send_ref[d * SLOTS + s]
                blk = src[jnp.minimum(pick, BLOCKS - 1)].astype(F32)
                fout[r, d, s] = jnp.where(pick < BLOCKS, blk, 0.0).astype(BF16)
        up = rcopy(fout.at[r, 1], fin.at[r, 0], fsend.at[r, 1], frecv.at[r, 0], above)
        dn = rcopy(fout.at[r, 0], fin.at[r, 1], fsend.at[r, 0], frecv.at[r, 1], below)
        up.start()
        dn.start()
        return up, dn

    def tile(t):
        for e in (2 * t, 2 * t + 1):
            extt_ref[e] = ext[e].T
        rhs = jnp.concatenate([ext[2 * t], ext[2 * t + 1]], axis=1)
        res = jnp.dot(w_ref[...], rhs, preferred_element_type=F32)
        prod[2 * t] = res[:, :BLOCK]
        prod[2 * t + 1] = res[:, BLOCK:]

    def part_tiles(i):
        def one(t, _):
            t = t + i * (CHUNK // 2) + (t // (CHUNK // 2)) * (CHUNK // 2)
            for r_abs, src in quarters:
                rows = rows_of(r_abs)
                ext[2 * t, rows, :] = src[2 * t]
                ext[2 * t + 1, rows, :] = src[2 * t + 1]
            tile(t)
            return 0

        lax.fori_loop(0, CHUNK, one, 0)

    copies = [pack(0, own)]
    prod[EXT] = jnp.zeros((OFFSETS * LOC, BLOCK), F32)
    extt_ref[EXT] = jnp.zeros((BLOCK, CH), BF16)
    low = lax.broadcasted_iota(jnp.int32, (LOC, BLOCK), 1) < LOC
    for p in range(WPAD // BLOCK):
        for h in range(2):
            cols = pl.ds(h * BLOCK, BLOCK)
            first = w_ref[pl.ds(2 * p * LOC, LOC), cols].astype(F32)
            if 2 * p + 1 < OFFSETS:
                second = w_ref[pl.ds((2 * p + 1) * LOC, LOC), cols].astype(F32)
            else:
                second = jnp.zeros((LOC, BLOCK), F32)
            put = pl.ds(p * BLOCK, BLOCK)
            parts_ref[2 * h, :, put] = jnp.where(low, first, pltpu.roll(second, LOC, 1)).astype(BF16)
            parts_ref[2 * h + 1, :, put] = jnp.where(low, pltpu.roll(first, LOC, 1), second).astype(BF16)
    gather.forward(0)
    gather.forward(1)
    gather.wait_part(0)
    part_tiles(0)
    gather.wait_part(1)
    copies.append(pack(1, from_dn))
    copies.append(pack(2, from_up))
    copies.append(pack(3, opp))
    part_tiles(1)
    keep_below = jnp.where(b > 0, 1.0, 0.0)
    keep_above = jnp.where(b < NBOX - 1, 1.0, 0.0)
    for r, (r_abs, _) in enumerate(quarters):
        up, dn = copies[r]
        up.wait_recv()
        dn.wait_recv()
        rows = rows_of(r_abs)
        for s in range(SLOTS):
            ext[BLOCKS + s, rows, :] = (fin[r, 0, s].astype(F32) * keep_below).astype(BF16)
            ext[BLOCKS + SLOTS + s, rows, :] = (fin[r, 1, s].astype(F32) * keep_above).astype(BF16)

    def face_tile(t, _):
        tile(t)
        return 0

    lax.fori_loop(BLOCKS // 2, EXT // 2, face_tile, 0)

    def out(j, carry):
        a, s = carry
        acc = prod[map_ref[j], pl.ds(0, LOC), :]
        for k in range(1, OFFSETS):
            acc = acc + prod[map_ref[k * BLOCKS + j], pl.ds(LOC * k, LOC), :]
        conv_ref[j] = acc
        o = occ_ref[j] * acc
        return a + o, s + o * acc

    zero = jnp.zeros((LOC, BLOCK), F32)
    a, s = lax.fori_loop(0, BLOCKS, out, (zero, zero))
    sum_ref[0] = a
    sum_ref[1] = s
    gather.wait_sends()
    for up, dn in copies:
        up.wait_send()
        dn.wait_send()


def conv_call(send, kmap, features, occ, w):
    quarter = pltpu.VMEM((BLOCKS, LOC, BLOCK), BF16)
    faces = pltpu.VMEM((4, 2, SLOTS, LOC, BLOCK), BF16)
    dma = pltpu.SemaphoreType.DMA
    return pl.pallas_call(
        conv_kernel,
        out_shape=(
            jax.ShapeDtypeStruct((BLOCKS, LOC, BLOCK), F32),
            jax.ShapeDtypeStruct((2, LOC, BLOCK), F32),
            jax.ShapeDtypeStruct((EXT + 1, BLOCK, CH), BF16),
            jax.ShapeDtypeStruct((4, LOC, WPAD), BF16),
        ),
        in_specs=[SMEM, SMEM, VMEM, VMEM, VMEM],
        out_specs=(VMEM,) * 4,
        scratch_shapes=[
            quarter,
            quarter,
            quarter,
            quarter,
            faces,
            faces,
            pltpu.VMEM((EXT, CH, BLOCK), BF16),
            pltpu.VMEM((EXT + 1, OFFSETS * LOC, BLOCK), F32),
            dma((12,)),
            dma((12,)),
            dma((4, 2)),
            dma((4, 2)),
        ],
        compiler_params=params(1),
        name="conv",
    )(send, kmap, features, occ, w)


def lane_masks():
    ch = lax.broadcasted_iota(jnp.int32, (LOC, BLOCK), 0)
    lane = lax.broadcasted_iota(jnp.int32, (LOC, BLOCK), 1)
    return lane == ch, lane == ch + LOC


def to_row(first, second):
    m0, m1 = lane_masks()
    c0 = jnp.sum(first, axis=1, keepdims=True)
    c1 = jnp.sum(second, axis=1, keepdims=True)
    return jnp.sum(jnp.where(m0, c0, 0.0) + jnp.where(m1, c1, 0.0), axis=0, keepdims=True)


def to_cols(row):
    m0, m1 = lane_masks()
    return (
        jnp.sum(jnp.where(m0, row, 0.0), axis=1, keepdims=True),
        jnp.sum(jnp.where(m1, row, 0.0), axis=1, keepdims=True),
    )


def at_box(x, z, core):
    return {"box": x * 16 + z * 2 + core}


def box_groups():
    b = lax.axis_index("box")
    x, z, core = b // 16, lax.rem(b // 2, 8), lax.rem(b, 2)
    first = [at_box(lax.rem(x + d // 2, 4), z, lax.rem(core + d % 2, 2)) for d in range(1, 8)]
    second = [at_box(x, lax.rem(z + d, 8), core) for d in range(1, 8)]
    return (x * 2 + core, first), (z, second)


def box_sum(mine, buf, ssem, rsem, idle=None):
    sent = []
    for step, (me, peers) in enumerate(box_groups()):
        buf[step, me] = mine
        copies = []
        for d, dev in enumerate(peers):
            c = rcopy(buf.at[step, me], buf.at[step, me], ssem.at[step, d], rsem.at[step, d], dev)
            c.start()
            copies.append(c)
        if idle is not None and step == 1:
            idle()
        for c in copies:
            c.wait_recv()
        mine = buf[step, 0]
        for d in range(1, 8):
            mine = mine + buf[step, d]
        sent += copies
    return mine, sent


def norm_kernel(
    map_ref,
    conv_ref,
    sum_ref,
    grad_ref,
    occ_ref,
    gs_ref,
    extt_ref,
    parts_ref,
    out_ref,
    cga_ref,
    wg_ref,
    stat_ref,
    win_ref,
    wrecv,
    normed,
    rgrad,
    own,
    from_dn,
    from_up,
    opp,
    sbuf,
    sbuf2,
    ysend,
    yrecv,
    ssend,
    srecv,
    wsend,
    wrecvs,
):
    q = lax.axis_index("ch")
    gather = YGather(own, from_dn, from_up, opp, ysend, yrecv)
    (_, near), (_, far) = box_groups()
    sub = lax.broadcasted_iota(jnp.int32, (2, BLOCK), 0)
    count = jnp.sum(occ_ref[...], axis=0)
    count = jnp.broadcast_to(jnp.sum(count, axis=1, keepdims=True), (1, BLOCK))
    row = to_row(sum_ref[0], sum_ref[1])
    pay = jnp.where(sub == 0, row, count)
    ypeers = [{"ch": lax.rem(q + d, 4)} for d in range(1, 4)]
    greet(ypeers + near + far)
    wcopies = []
    for d in range(1, 4):
        c = rcopy(parts_ref.at[lax.rem(q + d, 4)], wrecv.at[rows_of(q)], wsend.at[d - 1], wrecvs.at[d - 1], ypeers[d - 1])
        c.start()
        wcopies.append(c)
    wrecv[rows_of(q), :] = parts_ref[q]
    tot, sent = box_sum(pay, sbuf, ssend.at[0], srecv.at[0])
    n_vox = tot[1:2, 0:1]
    s1, s2 = to_cols(tot[0:1, :])
    mean = s1 / n_vox
    var = s2 / n_vox - mean * mean
    inv = 1.0 / jnp.sqrt(var + 1e-05)
    gain, shift = to_cols(gs_ref[...])

    def fwd(j, carry):
        a, b = carry
        cols = pl.ds(pl.multiple_of(j * BLOCK, BLOCK), BLOCK)
        occ = occ_ref[j]
        nd = (conv_ref[j] - mean) * inv
        sh = nd * gain + shift
        out_ref[:, cols] = (occ * jnp.maximum(sh, 0.0)).astype(BF16)
        rg = jnp.where(sh > 0.0, occ * grad_ref[:, cols].astype(F32), 0.0)
        normed[j] = nd
        rgrad[j] = rg
        return a + rg, b + rg * nd

    zero = jnp.zeros((LOC, BLOCK), F32)
    a, b = lax.fori_loop(0, BLOCKS, fwd, (zero, zero))
    row = to_row(a, b)

    def turn():
        for c in wcopies:
            c.wait_recv()
        for p in range(WPAD // BLOCK):
            win_ref[pl.ds(p * BLOCK, BLOCK), :] = wrecv[:, pl.ds(p * BLOCK, BLOCK)].T

    tot, sent2 = box_sum(row, sbuf2, ssend.at[1], srecv.at[1], turn)
    stat_ref[...] = tot
    sg, gg = to_cols(tot)
    scale = inv * gain
    sgm = sg / n_vox

    def bwd(j, _):
        nd = normed[j]
        own[j] = (occ_ref[j] * scale * (rgrad[j] - sgm - nd * gg / n_vox)).astype(BF16)
        return 0

    lax.fori_loop(0, BLOCKS, bwd, 0)
    gather.start()

    def kterm(k, _):
        lhs = jnp.concatenate([own[j] for j in range(BLOCKS)], axis=1)
        rhs = jnp.concatenate([extt_ref[map_ref[k * BLOCKS + j]] for j in range(BLOCKS)], axis=0)
        wg_ref[k] = jnp.dot(lhs, rhs, preferred_element_type=F32)
        return 0

    def place(r_abs, src):
        rows = rows_of(r_abs)

        def one(e, _):
            cga_ref[e, rows, :] = src[e]
            return 0

        lax.fori_loop(0, BLOCKS, one, 0)

    place(q, own)
    lax.fori_loop(0, 8, kterm, 0)
    gather.forward(0)
    lax.fori_loop(8, 14, kterm, 0)
    gather.forward(1)
    lax.fori_loop(14, OFFSETS, kterm, 0)
    gather.wait_part(0)
    gather.wait_part(1)
    place(lax.rem(q + 3, 4), from_dn)
    place(lax.rem(q + 1, 4), from_up)
    place(lax.rem(q + 2, 4), opp)
    gather.wait_sends()
    for c in wcopies + sent + sent2:
        c.wait_send()


def norm_call(kmap, conv, sums, out_grad, occ, gs, extt, parts):
    quarter = pltpu.VMEM((BLOCKS, LOC, BLOCK), BF16)
    return pl.pallas_call(
        norm_kernel,
        out_shape=(
            jax.ShapeDtypeStruct((LOC, BLOCKS * BLOCK), BF16),
            jax.ShapeDtypeStruct((BLOCKS, CH, BLOCK), BF16),
            jax.ShapeDtypeStruct((OFFSETS, LOC, CH), F32),
            jax.ShapeDtypeStruct((1, BLOCK), F32),
            jax.ShapeDtypeStruct((WPAD, CH), BF16),
        ),
        in_specs=[SMEM] + [VMEM] * 7,
        out_specs=(VMEM,) * 5,
        scratch_shapes=[
            pltpu.VMEM((CH, WPAD), BF16),
            pltpu.VMEM((BLOCKS, LOC, BLOCK), F32),
            pltpu.VMEM((BLOCKS, LOC, BLOCK), F32),
            quarter,
            quarter,
            quarter,
            quarter,
            pltpu.VMEM((2, 8, 2, BLOCK), F32),
            pltpu.VMEM((2, 8, 1, BLOCK), F32),
            pltpu.SemaphoreType.DMA((12,)),
            pltpu.SemaphoreType.DMA((12,)),
            pltpu.SemaphoreType.DMA((2, 2, 7)),
            pltpu.SemaphoreType.DMA((2, 2, 7)),
            pltpu.SemaphoreType.DMA((3,)),
            pltpu.SemaphoreType.DMA((3,)),
        ],
        compiler_params=params(2),
        name="norm",
    )(kmap, conv, sums, out_grad, occ, gs, extt, parts)


def back_kernel(map_ref, w_ref, cg_ref, eg_ref, prod, *accs):
    for a in accs:

        def zero(e, _):
            a[e] = jnp.zeros((LOC, BLOCK), F32)
            return 0

        lax.fori_loop(0, EXT + 1, zero, 0)

    def tile(t, _):
        rhs = jnp.concatenate([cg_ref[2 * t], cg_ref[2 * t + 1]], axis=1)
        res = jnp.dot(w_ref[pl.ds(0, OFFSETS * LOC), :], rhs, preferred_element_type=F32)
        prod[2 * t] = res[:, :BLOCK]
        prod[2 * t + 1] = res[:, BLOCK:]
        return 0

    lax.fori_loop(0, BLOCKS // 2, tile, 0)

    def scatter(t, _):
        for k in range(OFFSETS):
            at = [map_ref[k * BLOCKS + t * NA + i] for i in range(NA)]
            new = [accs[i][at[i]] + prod[t * NA + i, pl.ds(LOC * k, LOC), :] for i in range(NA)]
            for i in range(NA):
                accs[i][at[i]] = new[i]
        return 0

    lax.fori_loop(0, BLOCKS // NA, scatter, 0)

    def finish(e, _):
        s = accs[0][e]
        for a in accs[1:]:
            s = s + a[e]
        eg_ref[e] = s
        return 0

    lax.fori_loop(0, EXT, finish, 0)


def back_call(kmap, w, cga):
    return pl.pallas_call(
        back_kernel,
        out_shape=jax.ShapeDtypeStruct((EXT, LOC, BLOCK), F32),
        in_specs=[SMEM, VMEM, VMEM],
        out_specs=VMEM,
        scratch_shapes=[pltpu.VMEM((BLOCKS, OFFSETS * LOC, BLOCK), F32)]
        + [pltpu.VMEM((EXT + 1, LOC, BLOCK), F32)] * NA,
        compiler_params=params(),
        name="back",
    )(kmap, w, cga)


def final_kernel(
    send_ref,
    eg_ref,
    occ_ref,
    wg_ref,
    in_ref,
    wout_ref,
    fout,
    fin,
    give,
    given,
    keep,
    xbuf,
    xin,
    zbuf,
    zin,
    res,
    fsend,
    frecv,
    sem,
    sems,
):
    b = lax.axis_index("box")
    x, z, core = b // 16, lax.rem(b // 2, 8), lax.rem(b, 2)
    above = {"box": lax.rem(b + 1, NBOX)}
    below = {"box": lax.rem(b + NBOX - 1, NBOX)}
    mate = at_box(x, z, 1 - core)
    zpeers = [at_box(x, lax.rem(z + d, 8), core) for d in range(1, 8)]
    xpeers = [at_box(lax.rem(x + d, 4), z, core) for d in range(1, 4)]
    sent = []

    def send(src, dst, i, dev):
        c = rcopy(src, dst, sem.at[i], sems.at[i], dev)
        c.start()
        sent.append(c)
        return c

    def cut(k, _):
        rows = pl.ds(pl.multiple_of(k * LOC, LOC), LOC)
        lo, hi = wg_ref[k, :, :BLOCK], wg_ref[k, :, BLOCK:]
        keep[rows, :] = jnp.where(core == 0, lo, hi)
        give[rows, :] = jnp.where(core == 0, hi, lo).astype(BF16)
        return 0

    lax.fori_loop(0, OFFSETS, cut, 0)
    for s in range(SLOTS):
        fout[0, s] = eg_ref[BLOCKS + s].astype(BF16)
        fout[1, s] = eg_ref[BLOCKS + SLOTS + s].astype(BF16)
    greet([above, below, mate] + zpeers + xpeers)
    pair = send(give, given, 0, mate)
    f0 = rcopy(fout.at[0], fin.at[0], fsend.at[0], frecv.at[0], below)
    f1 = rcopy(fout.at[1], fin.at[1], fsend.at[1], frecv.at[1], above)
    f0.start()
    f1.start()
    sent += [f0, f1]
    xbuf[pl.ds(OFFSETS * LOC, WROWS - OFFSETS * LOC), :] = jnp.zeros((WROWS - OFFSETS * LOC, BLOCK), BF16)
    pair.wait_recv()

    def add(k, _):
        rows = pl.ds(pl.multiple_of(k * LOC, LOC), LOC)
        xbuf[rows, :] = (keep[rows, :] + given[rows, :].astype(F32)).astype(BF16)
        return 0

    lax.fori_loop(0, OFFSETS, add, 0)
    xpart = lambda i: pl.ds(pl.multiple_of(i * XROWS, XROWS), XROWS)
    zpart = lambda i: pl.ds(pl.multiple_of(i * ZROWS, ZROWS), ZROWS)
    xc = [send(xbuf.at[xpart(lax.rem(x + d, 4))], xin.at[d - 1], d, xpeers[d - 1]) for d in range(1, 4)]
    for c in xc:
        c.wait_recv()
    tot = xbuf[xpart(x), :].astype(F32)
    for d in range(3):
        tot = tot + xin[d].astype(F32)
    zbuf[...] = tot.astype(BF16)
    zc = [send(zbuf.at[zpart(lax.rem(z + d, 8))], zin.at[d - 1], 3 + d, zpeers[d - 1]) for d in range(1, 8)]

    f0.wait_recv()
    f1.wait_recv()
    up_ok = b < NBOX - 1
    dn_ok = b > 0

    def settle(d, _):
        t = eg_ref[d]
        for s in range(SLOTS):
            t = t + jnp.where((send_ref[SLOTS + s] == d) & up_ok, fin[0, s].astype(F32), 0.0)
            t = t + jnp.where((send_ref[s] == d) & dn_ok, fin[1, s].astype(F32), 0.0)
        in_ref[:, pl.ds(pl.multiple_of(d * BLOCK, BLOCK), BLOCK)] = (occ_ref[d] * t).astype(BF16)
        return 0

    lax.fori_loop(0, BLOCKS, settle, 0)

    for c in zc:
        c.wait_recv()
    tot = zbuf[zpart(z), :].astype(F32)
    for d in range(7):
        tot = tot + zin[d].astype(F32)
    mine = pl.ds(pl.multiple_of(x * XROWS + z * ZROWS, ZROWS), ZROWS)
    res[0, mine, :] = tot.astype(BF16)
    zc = [send(res.at[0, mine], res.at[0, mine], 10 + d, zpeers[d - 1]) for d in range(1, 8)]
    for c in zc:
        c.wait_recv()
    xc = [send(res.at[0, xpart(x)], res.at[0, xpart(x)], 17 + d, xpeers[d - 1]) for d in range(1, 4)]
    for c in xc:
        c.wait_recv()
    valid = pl.ds(0, OFFSETS * LOC)
    pair = send(res.at[0, valid], res.at[1, valid], 21, mate)
    pair.wait_recv()

    def put(k, _):
        r = pl.ds(pl.multiple_of(k * LOC, LOC), LOC)
        m = res[0, r, :].astype(F32)
        o = res[1, r, :].astype(F32)
        wout_ref[k, :, :BLOCK] = jnp.where(core == 0, m, o)
        wout_ref[k, :, BLOCK:] = jnp.where(core == 0, o, m)
        return 0

    lax.fori_loop(0, OFFSETS, put, 0)
    for c in sent:
        c.wait_send()


def final_call(send, eg, occ, wg):
    dma = pltpu.SemaphoreType.DMA
    return pl.pallas_call(
        final_kernel,
        out_shape=(
            jax.ShapeDtypeStruct((LOC, BLOCKS * BLOCK), BF16),
            jax.ShapeDtypeStruct((OFFSETS, LOC, CH), F32),
        ),
        in_specs=[SMEM, VMEM, VMEM, VMEM],
        out_specs=(VMEM, VMEM),
        scratch_shapes=[
            pltpu.VMEM((2, SLOTS, LOC, BLOCK), BF16),
            pltpu.VMEM((2, SLOTS, LOC, BLOCK), BF16),
            pltpu.VMEM((OFFSETS * LOC, BLOCK), BF16),
            pltpu.VMEM((OFFSETS * LOC, BLOCK), BF16),
            pltpu.VMEM((OFFSETS * LOC, BLOCK), F32),
            pltpu.VMEM((WROWS, BLOCK), BF16),
            pltpu.VMEM((3, XROWS, BLOCK), BF16),
            pltpu.VMEM((XROWS, BLOCK), BF16),
            pltpu.VMEM((7, ZROWS, BLOCK), BF16),
            pltpu.VMEM((2, WROWS, BLOCK), BF16),
            dma((2,)),
            dma((2,)),
            dma((22,)),
            dma((22,)),
        ],
        compiler_params=params(3),
        name="final",
    )(send, eg, occ, wg)


def per_device(
    features, occupied, send_lists, kernel_map, weights, norm_gain, norm_shift, out_grad
):
    occ = occupied.astype(F32).reshape(BLOCKS, 1, BLOCK)
    send = send_lists.reshape(2 * SLOTS)
    kmap = kernel_map.reshape(OFFSETS * BLOCKS)
    w = weights.reshape(OFFSETS * LOC, CH)
    gs = jnp.concatenate([norm_gain, norm_shift]).reshape(1, BLOCK)

    conv, sums, extt, parts = conv_call(send, kmap, features, occ, w)
    out_features, cga, wg, stat, w_in = norm_call(kmap, conv, sums, out_grad, occ, gs, extt, parts)
    eg = back_call(kmap, w_in, cga)
    in_grad, weight_grad = final_call(send, eg, occ, wg)
    return (out_features, in_grad, weight_grad, stat[0, LOC:], stat[0, :LOC])


def solution(mesh):
    in_specs = (
        P("ch", "box"),
        P("box"),
        P("box", None, None),
        P("box", None, None),
        P(None, "ch", None),
        P("ch"),
        P("ch"),
        P("ch", "box"),
    )
    out_specs = (P("ch", "box"), P("ch", "box"), P(None, "ch", None), P("ch"), P("ch"))
    return jax.shard_map(
        per_device, mesh=mesh, in_specs=in_specs, out_specs=out_specs, check_vma=False
    )
```

time: 211 us -> 157 us (0.74)
  Pallas kernels: 185 us -> 145 us
  local copies, waits for them, and re-layouts: 19 us -> 7.16 us
  starting transfers between devices: 5.01 us -> 0 us
    pallas_call x1 -> x0, Pallas kernels: 35.4 us -> none  [make_ext(): pl.pallas_call(ext_kernel, out_shape=jax.ShapeDtypeStruct((EXT + 1, CH, B...]
    pallas_call x1, Pallas kernels: 23.1 us -> 40.7 us  [conv_call(): pl.pallas_call(conv_kernel, out_shape=(jax.ShapeDtypeStruct((BLOCKS, LOC,...]
    pallas_call x1, Pallas kernels: 64.1 us -> 51.3 us  [norm_call(): pl.pallas_call(norm_kernel, out_shape=(jax.ShapeDtypeStruct((LOC, BLOCKS...]
    pallas_call x1, Pallas kernels: 19.2 us -> 13.9 us  [back_call(): pl.pallas_call(back_kernel, out_shape=jax.ShapeDtypeStruct((EXT, LOC, BLO...]
    all_to_all x1 -> x0, starting transfers between devices: 5.01 us -> none  [per_device(): whole = lax.all_to_all(parts, 'ch', split_axis=0, concat_axis=0)]
    reshape x2 -> x0, local copies, waits for them, and re-layouts: 4.87 us -> none  [the longest x1 2.97 us: per_device(): parts = weights.reshape(OFFSETS, LOC, 4, LOC).transpose(2, 0, 3, 1)]
    transpose x2 -> x0, local copies, waits for them, and re-layouts: 3.94 us -> none  [the longest x1 2.31 us: per_device(): parts = weights.reshape(OFFSETS, LOC, 4, LOC).transpose(2, 0, 3, 1)]
    unnamed x19 -> x7, local copies, waits for them, and re-layouts: 7.73 us -> 3.88 us
  transfers between devices with their start and end apart: 1 -> 0, of which waited for: 0 -> 0; matrix products, arithmetic and copies ran while one was open for 2% -> 0% of each run, Pallas kernels for 58% -> 0%
where the time goes in v2:
time: 157 us; the launch traced here: 156 us
  Pallas kernels  145 us (92%)
  local copies, waits for them, and re-layouts  7.16 us (5%)
  other arithmetic  3.33 us (2%)
    pallas_call x1, Pallas kernels, norm_call(): pl.pallas_call(norm_kernel, out_shape=(jax.ShapeDtypeStruct((LOC, BLOCKS...  51.3 us
    pallas_call x1, Pallas kernels, conv_call(): pl.pallas_call(conv_kernel, out_shape=(jax.ShapeDtypeStruct((BLOCKS, LOC,...  40.7 us
    pallas_call x1, Pallas kernels, final_call(): pl.pallas_call(final_kernel, out_shape=(jax.ShapeDtypeStruct((LOC, BLOCKS...  39.2 us
    pallas_call x1, Pallas kernels, back_call(): pl.pallas_call(back_kernel, out_shape=jax.ShapeDtypeStruct((EXT, LOC, BLO...  13.9 us
    unnamed x7, local copies, waits for them, and re-layouts  3.88 us

profile of v2, /device:TPU:1, one launch (start us, length us, event | category | flops | bytes accessed | tf_op | source)
XLA Modules:
  0.0 156.3 jit_solution(13991966501003937410)
XLA Ops:
  0.6 1.3 reshape.26.send_ref
  2.0 1.3 maximum_bitcast_fusion.gs_ref
  3.2 1.3 convert_element_type.3
  4.6 0.8 reduce
  5.3 0.7 reshape.25.map_ref
  6.0 40.7 %conv.1 = (f32[32,64,128]{2,1,0:T(8,128)}, f32[2,64,128]{2,1,0:T(8,128)}, bf16[49,128,256]{2,1,0:T(8,128)(2,1)}, bf16[4,64,1792]{2,1,0:T(8,128)(2,1)}) custom-call(s32[16]{0:T(128)} %reshape.26.send_ref, s32[864]{0:T(1024)} %reshape.25.map_ref, bf16[64,4096]{1,0:T(8,128)(2,1)} %feat_ref.1, f32[32,1,128]{2,1,0:T(1,128)} %bitcast.9, bf16[1728,256]{1,0:T(8,128)(2,1)} %bitcast.8), custom_call_target="tpu_custom_call" | custom-call | tf_op jit(solution)/shard_map/conv/pallas_call | solution.py:233
  46.7 51.3 %norm.1 = (bf16[64,4096]{1,0:T(8,128)(2,1)}, bf16[32,256,128]{2,1,0:T(8,128)(2,1)}, f32[27,64,256]{2,1,0:T(8,128)}, f32[1,128]{1,0:T(1,128)}, bf16[1792,256]{1,0:T(8,128)(2,1)}) custom-call(s32[864]{0:T(1024)} %reshape.25.map_ref, f32[32,64,128]{2,1,0:T(8,128)} %get-tuple-element.16.conv_ref, f32[2,64,128]{2,1,0:T(8,128)} %get-tuple-element.17.sum_ref, ...), custom_call_target="tpu_custom_call" | custom-call | tf_op jit(solution)/shard_map/norm/pallas_call | solution.py:438
  98.0 1.3 slice_bitcast_fusion
  99.3 13.9 %back.1.eg_ref = f32[48,64,128]{2,1,0:T(8,128)} custom-call(s32[864]{0:T(1024)} %reshape.25.map_ref, bf16[1792,256]{1,0:T(8,128)(2,1)} %get-tuple-element.21.w_ref, bf16[32,256,128]{2,1,0:T(8,128)(2,1)} %get-tuple-element.22.cg_ref), custom_call_target="tpu_custom_call" | custom-call | tf_op jit(solution)/shard_map/back/pallas_call | solution.py:510
  113.2 0.0 copy-start.1
  113.2 39.2 %final.1 = (bf16[64,4096]{1,0:T(8,128)(2,1)}, f32[27,64,256]{2,1,0:T(8,128)}) custom-call(s32[16]{0:T(128)} %reshape.26.send_ref, f32[48,64,128]{2,1,0:T(8,128)} %back.1.eg_ref, f32[32,1,128]{2,1,0:T(1,128)} %bitcast.11, f32[27,64,256]{2,1,0:T(8,128)} %get-tuple-element.23.wg_ref), custom_call_target="tpu_custom_call" | custom-call | tf_op jit(solution)/shard_map/final/pallas_call | solution.py:644
  152.4 0.0 copy-start
  152.4 0.0 copy-done.1
  152.4 0.8 copy.16
  153.2 1.9 %copy.17 = bf16[64,4096]{1,0:T(8,128)(2,1)} copy(bf16[64,4096]{1,0:T(8,128)(2,1)} %get-tuple-element.35) | data formatting | bytes 1048576
  155.1 0.0 copy-done
  155.1 1.2 copy.18
Async XLA Ops:
  113.2 39.2 %copy-start.1 = (bf16[64,4096]{1,0:T(8,128)(2,1)S(1)}, bf16[64,4096]{1,0:T(8,128)(2,1)}, u32[]{:S(2)}) copy-start(bf16[64,4096]{1,0:T(8,128)(2,1)} %get-tuple-element.34) | copy-start | bytes 1572868
  152.4 2.7 %copy-start = (f32[27,64,256]{2,1,0:T(8,128)S(1)}, f32[27,64,256]{2,1,0:T(8,128)}, u32[]{:S(2)}) copy-start(f32[27,64,256]{2,1,0:T(8,128)} %get-tuple-element.36) | copy-start | bytes 5308420

commit v3 on v2

v3 whole, which is shorter than its diff:
```python
import functools

import jax
import jax.numpy as jnp
from jax import lax
from jax.experimental import pallas as pl
from jax.experimental.pallas import tpu as pltpu
from jax.sharding import PartitionSpec as P

F32 = jnp.float32
BF16 = jnp.bfloat16
MESH = pl.DeviceIdType.MESH
VMEM = pl.BlockSpec(memory_space=pltpu.VMEM)
SMEM = pl.BlockSpec(memory_space=pltpu.SMEM)
VMEM_LIMIT = 62 * 2**20

BLOCK = 128
BLOCKS = 32
CHUNK = 8
SLOTS = 8
EXT = BLOCKS + 2 * SLOTS
OFFSETS = 27
CH = 256
LOC = 64
WPAD = 1792
KHALF = 14
KCOUNT = (14, 13)
WROWS = 1024
XROWS = WROWS // 4
ZROWS = XROWS // 8
NBOX = 64
HROWS = 32
WALK = 16


def params(cid=None):
    if cid is None:
        return pltpu.CompilerParams(vmem_limit_bytes=VMEM_LIMIT)
    return pltpu.CompilerParams(
        vmem_limit_bytes=VMEM_LIMIT, collective_id=cid, has_side_effects=True
    )


def rcopy(src, dst, ssem, rsem, dev):
    return pltpu.make_async_remote_copy(
        src_ref=src, dst_ref=dst, send_sem=ssem, recv_sem=rsem, device_id=dev, device_id_type=MESH
    )


def greet(devs):
    barrier = pltpu.get_barrier_semaphore()
    for dev in devs:
        pl.semaphore_signal(barrier, inc=1, device_id=dev, device_id_type=MESH)
    pl.semaphore_wait(barrier, len(devs))


def occ_of(occ_ref, j):
    return occ_ref[j].astype(F32)


def rows_of(q):
    return pl.ds(pl.multiple_of(q * LOC, LOC), LOC)


class YGather:
    def __init__(self, own, from_dn, from_up, opp, ssem, rsem):
        q = lax.axis_index("ch")
        self.up = {"ch": lax.rem(q + 1, 4)}
        self.dn = {"ch": lax.rem(q + 3, 4)}

        def mk(src, dst, chunk, i, dev):
            part = pl.ds(chunk * CHUNK, CHUNK)
            return rcopy(src.at[part], dst.at[part], ssem.at[i], rsem.at[i], dev)

        self.own_up = [mk(own, from_dn, c, c, self.up) for c in range(4)]
        self.own_dn = [mk(own, from_up, c, 4 + c, self.dn) for c in range(4)]
        self.far_up = [mk(from_dn, opp, c, 8 + c, self.up) for c in (0, 1)]
        self.far_dn = [mk(from_up, opp, c, 8 + c, self.dn) for c in (2, 3)]

    def start(self):
        self.own_up[0].start()
        self.own_dn[2].start()
        self.own_up[1].start()
        self.own_dn[3].start()

    def forward(self, i):
        self.own_up[i].wait_recv()
        self.far_up[i].start()
        self.own_up[2 + i].start()
        self.own_dn[2 + i].wait_recv()
        self.far_dn[i].start()
        self.own_dn[i].start()

    def wait_part(self, i):
        self.own_up[2 + i].wait_recv()
        self.own_dn[i].wait_recv()
        self.far_up[i].wait_recv()
        self.far_dn[i].wait_recv()

    def wait_sends(self):
        for c in self.own_up + self.own_dn + self.far_up + self.far_dn:
            c.wait_send()


def rank_pairs(map_ref):
    at = lax.broadcasted_iota(jnp.int32, (8, BLOCK), 0) * BLOCK + lax.broadcasted_iota(jnp.int32, (8, BLOCK), 1)

    def fill(k, target):
        for j in range(BLOCKS):
            target = jnp.where(at == k * BLOCKS + j, map_ref[0, k, j], target)
        return target

    target = lax.fori_loop(0, OFFSETS, fill, jnp.full((8, BLOCK), 63, jnp.int32))
    keys = target * 1024 + at

    def count(k, rank):
        for j in range(BLOCKS):
            rank = rank + (keys > map_ref[0, k, j] * 1024 + (k * BLOCKS + j)).astype(jnp.int32)
        return rank

    return target, lax.fori_loop(0, OFFSETS, count, jnp.zeros((8, BLOCK), jnp.int32))


def sort_pairs(target, rank):
    lane = lax.broadcasted_iota(jnp.int32, (BLOCK, BLOCK), 1)
    sub = lax.broadcasted_iota(jnp.int32, (BLOCK, BLOCK), 0)
    pair = [jnp.zeros((1, BLOCK), F32) for _ in range(7)]
    goal = [jnp.zeros((1, BLOCK), F32) for _ in range(7)]
    last = jnp.full((1, BLOCK), -1.0, F32)
    for s in range(7):
        rcol = jnp.broadcast_to(rank[s : s + 1, :].astype(F32), (BLOCK, BLOCK)).T
        tcol = jnp.broadcast_to(target[s : s + 1, :].astype(F32), (BLOCK, BLOCK)).T
        i = sub + s * BLOCK
        number = (lax.rem(i, BLOCKS) * (2 * OFFSETS) + 2 * (i // BLOCKS)).astype(F32)
        for r in range(7):
            hit = rcol == (lane + r * BLOCK).astype(F32)
            pair[r] = pair[r] + jnp.sum(jnp.where(hit, number, 0.0), axis=0, keepdims=True)
            goal[r] = goal[r] + jnp.sum(jnp.where(hit, tcol, 0.0), axis=0, keepdims=True)
        mine = tcol == lane.astype(F32)
        last = jnp.maximum(last, jnp.max(jnp.where(mine, rcol, -1.0), axis=0, keepdims=True))
    fresh = []
    first = lax.broadcasted_iota(jnp.int32, (1, BLOCK), 1) == 0
    for r in range(7):
        before = pltpu.roll(goal[r], 1, 1)
        carry = pltpu.roll(goal[r - 1], 1, 1) if r else jnp.full((1, BLOCK), -1.0, F32)
        before = jnp.where(first, carry, before)
        fresh.append(jnp.where(goal[r] == before, 0.0, 1.0))
    some = [jnp.where(last >= 0.0, 1.0, 0.0)]
    return jnp.concatenate(pair + [jnp.maximum(last, 0.0)] + fresh + some, axis=0).astype(jnp.int32)


def conv_kernel(
    send_ref,
    map_ref,
    feat_ref,
    occ_ref,
    w_ref,
    conv_ref,
    sum_ref,
    ext,
    parts_ref,
    meta_ref,
    own,
    from_dn,
    from_up,
    opp,
    fout,
    fin,
    prod,
    ysend,
    yrecv,
    fsend,
    frecv,
):
    q = lax.axis_index("ch")
    b = lax.axis_index("box")
    above = {"box": lax.rem(b + 1, NBOX)}
    below = {"box": lax.rem(b + NBOX - 1, NBOX)}
    gather = YGather(own, from_dn, from_up, opp, ysend, yrecv)
    quarters = ((q, own), (lax.rem(q + 3, 4), from_dn), (lax.rem(q + 1, 4), from_up), (lax.rem(q + 2, 4), opp))

    def mask(e, _):
        x = feat_ref[:, pl.ds(pl.multiple_of(e * BLOCK, BLOCK), BLOCK)].astype(F32)
        own[e] = (x * occ_of(occ_ref, e)).astype(BF16)
        return 0

    lax.fori_loop(0, BLOCKS, mask, 0)
    greet([gather.up, gather.dn, above, below])
    gather.start()

    def pack(r, src):
        for d in range(2):
            for s in range(SLOTS):
                pick = send_ref[0, d, s]
                blk = src[jnp.minimum(pick, BLOCKS - 1)].astype(F32)
                fout[r, d, s] = jnp.where(pick < BLOCKS, blk, 0.0).astype(BF16)
        up = rcopy(fout.at[r, 1], fin.at[r, 0], fsend.at[r, 1], frecv.at[r, 0], above)
        dn = rcopy(fout.at[r, 0], fin.at[r, 1], fsend.at[r, 0], frecv.at[r, 1], below)
        up.start()
        dn.start()
        return up, dn

    def tile(t):
        rhs = jnp.concatenate([ext[2 * t], ext[2 * t + 1]], axis=1)
        res = jnp.dot(w_ref[...], rhs, preferred_element_type=F32)
        prod[2 * t] = res[:, :BLOCK]
        prod[2 * t + 1] = res[:, BLOCK:]

    def part_tiles(i):
        def one(t, _):
            t = t + i * (CHUNK // 2) + (t // (CHUNK // 2)) * (CHUNK // 2)
            for r_abs, src in quarters:
                rows = rows_of(r_abs)
                ext[2 * t, rows, :] = src[2 * t]
                ext[2 * t + 1, rows, :] = src[2 * t + 1]
            tile(t)
            return 0

        lax.fori_loop(0, CHUNK, one, 0)

    copies = [pack(0, own)]
    prod[EXT] = jnp.zeros((OFFSETS * LOC, BLOCK), F32)
    ext[EXT] = jnp.zeros((CH, BLOCK), BF16)
    low = lax.broadcasted_iota(jnp.int32, (LOC, BLOCK), 1) < LOC
    for p in range(WPAD // BLOCK):
        for h in range(2):
            cols = pl.ds(h * BLOCK, BLOCK)
            first = w_ref[pl.ds(2 * p * LOC, LOC), cols].astype(F32)
            if 2 * p + 1 < OFFSETS:
                second = w_ref[pl.ds((2 * p + 1) * LOC, LOC), cols].astype(F32)
            else:
                second = jnp.zeros((LOC, BLOCK), F32)
            put = pl.ds(p * BLOCK, BLOCK)
            parts_ref[2 * h, :, put] = jnp.where(low, first, pltpu.roll(second, LOC, 1)).astype(BF16)
            parts_ref[2 * h + 1, :, put] = jnp.where(low, pltpu.roll(first, LOC, 1), second).astype(BF16)
    gather.forward(0)
    ranks = rank_pairs(map_ref)
    gather.forward(1)
    meta_ref[...] = sort_pairs(*ranks)
    gather.wait_part(0)
    part_tiles(0)
    gather.wait_part(1)
    copies.append(pack(1, from_dn))
    copies.append(pack(2, from_up))
    copies.append(pack(3, opp))
    part_tiles(1)
    keep_below = jnp.where(b > 0, 1.0, 0.0)
    keep_above = jnp.where(b < NBOX - 1, 1.0, 0.0)
    for r, (r_abs, _) in enumerate(quarters):
        up, dn = copies[r]
        up.wait_recv()
        dn.wait_recv()
        rows = rows_of(r_abs)
        for s in range(SLOTS):
            ext[BLOCKS + s, rows, :] = (fin[r, 0, s].astype(F32) * keep_below).astype(BF16)
            ext[BLOCKS + SLOTS + s, rows, :] = (fin[r, 1, s].astype(F32) * keep_above).astype(BF16)

    def face_tile(t, _):
        tile(t)
        return 0

    lax.fori_loop(BLOCKS // 2, EXT // 2, face_tile, 0)

    def out(j, carry):
        a, s = carry
        acc = prod[map_ref[0, 0, j], pl.ds(0, LOC), :]
        for k in range(1, OFFSETS):
            acc = acc + prod[map_ref[0, k, j], pl.ds(LOC * k, LOC), :]
        conv_ref[j] = acc
        o = occ_of(occ_ref, j) * acc
        return a + o, s + o * acc

    zero = jnp.zeros((LOC, BLOCK), F32)
    a, s = lax.fori_loop(0, BLOCKS, out, (zero, zero))
    sum_ref[0] = a
    sum_ref[1] = s
    gather.wait_sends()
    for up, dn in copies:
        up.wait_send()
        dn.wait_send()


def conv_call(send, kmap, features, occ, w):
    quarter = pltpu.VMEM((BLOCKS, LOC, BLOCK), BF16)
    faces = pltpu.VMEM((4, 2, SLOTS, LOC, BLOCK), BF16)
    dma = pltpu.SemaphoreType.DMA
    return pl.pallas_call(
        conv_kernel,
        out_shape=(
            jax.ShapeDtypeStruct((BLOCKS, LOC, BLOCK), F32),
            jax.ShapeDtypeStruct((2, LOC, BLOCK), F32),
            jax.ShapeDtypeStruct((EXT + 1, CH, BLOCK), BF16),
            jax.ShapeDtypeStruct((4, LOC, WPAD), BF16),
            jax.ShapeDtypeStruct((16, BLOCK), jnp.int32),
        ),
        in_specs=[SMEM, SMEM, VMEM, VMEM, VMEM],
        out_specs=(VMEM,) * 5,
        scratch_shapes=[
            quarter,
            quarter,
            quarter,
            quarter,
            faces,
            faces,
            pltpu.VMEM((EXT + 1, OFFSETS * LOC, BLOCK), F32),
            dma((12,)),
            dma((12,)),
            dma((4, 2)),
            dma((4, 2)),
        ],
        compiler_params=params(1),
        name="conv",
    )(send, kmap, features, occ, w)


def lane_masks():
    ch = lax.broadcasted_iota(jnp.int32, (LOC, BLOCK), 0)
    lane = lax.broadcasted_iota(jnp.int32, (LOC, BLOCK), 1)
    return lane == ch, lane == ch + LOC


def to_row(first, second):
    m0, m1 = lane_masks()
    c0 = jnp.sum(first, axis=1, keepdims=True)
    c1 = jnp.sum(second, axis=1, keepdims=True)
    return jnp.sum(jnp.where(m0, c0, 0.0) + jnp.where(m1, c1, 0.0), axis=0, keepdims=True)


def to_cols(row):
    m0, m1 = lane_masks()
    return (
        jnp.sum(jnp.where(m0, row, 0.0), axis=1, keepdims=True),
        jnp.sum(jnp.where(m1, row, 0.0), axis=1, keepdims=True),
    )


def at_box(x, z, core):
    return {"box": x * 16 + z * 2 + core}


def to_col(row):
    ch = lax.broadcasted_iota(jnp.int32, (LOC, LOC), 0)
    lane = lax.broadcasted_iota(jnp.int32, (LOC, LOC), 1)
    return jnp.sum(jnp.where(ch == lane, row, 0.0), axis=1, keepdims=True)


def box_groups():
    b = lax.axis_index("box")
    x, z, core = b // 16, lax.rem(b // 2, 8), lax.rem(b, 2)
    first = [at_box(lax.rem(x + d // 2, 4), z, lax.rem(core + d % 2, 2)) for d in range(1, 8)]
    second = [at_box(x, lax.rem(z + d, 8), core) for d in range(1, 8)]
    return (x * 2 + core, first), (z, second)


def box_sum(mine, buf, ssem, rsem, idle):
    sent = []
    for step, (me, peers) in enumerate(box_groups()):
        buf[step, me] = mine
        copies = []
        for d, dev in enumerate(peers):
            c = rcopy(buf.at[step, me], buf.at[step, me], ssem.at[step, d], rsem.at[step, d], dev)
            c.start()
            copies.append(c)
        idle(step)
        for c in copies:
            c.wait_recv()
        mine = buf[step, 0]
        for d in range(1, 8):
            mine = mine + buf[step, d]
        sent += copies
    return mine, sent


def norm_kernel(
    send_ref,
    map_ref,
    meta_ref,
    conv_ref,
    sum_ref,
    grad_ref,
    occ_ref,
    gain_ref,
    shift_ref,
    ext_ref,
    parts_ref,
    out_ref,
    in_ref,
    wout_ref,
    stat_ref,
    extt,
    wg,
    wrecv,
    win,
    prod,
    run,
    eg,
    own,
    from_dn,
    from_up,
    opp,
    sbuf,
    sbuf2,
    fout,
    fin,
    give,
    given,
    xbuf,
    xin,
    zbuf,
    zin,
    res,
    ysend,
    yrecv,
    ssend,
    srecv,
    wsend,
    wrecvs,
    fsend,
    frecv,
    gsend,
    grecv,
):
    q = lax.axis_index("ch")
    b = lax.axis_index("box")
    x, z, core = b // 16, lax.rem(b // 2, 8), lax.rem(b, 2)
    gather = YGather(own, from_dn, from_up, opp, ysend, yrecv)
    (_, near), (_, far) = box_groups()
    ypeers = [{"ch": lax.rem(q + d, 4)} for d in range(1, 4)]
    above = {"box": lax.rem(b + 1, NBOX)}
    below = {"box": lax.rem(b + NBOX - 1, NBOX)}
    mate = at_box(x, z, 1 - core)
    xpeers = [at_box(lax.rem(x + d, 4), z, core) for d in range(1, 4)]
    zpeers = far
    sent = []

    count = jnp.sum(occ_ref[...].astype(F32), axis=0)
    count = jnp.broadcast_to(jnp.sum(count, axis=1, keepdims=True), (1, BLOCK))
    row = to_row(sum_ref[0], sum_ref[1])
    sub = lax.broadcasted_iota(jnp.int32, (2, BLOCK), 0)
    pay = jnp.where(sub == 0, row, count)
    greet(ypeers + near + far + [above, below])
    wcopies = []
    for d, slot in ((1, 1), (3, 2), (2, 3)):
        dst = wrecv.at[pl.ds(slot * LOC, LOC)]
        c = rcopy(parts_ref.at[lax.rem(q + d, 4)], dst, wsend.at[d - 1], wrecvs.at[d - 1], ypeers[d - 1])
        c.start()
        wcopies.append(c)
    wrecv[pl.ds(0, LOC), :] = parts_ref[q]

    def flip(step):
        def one(e, _):
            extt[e] = ext_ref[e].T
            return 0

        lax.fori_loop(*((0, EXT // 2) if step == 0 else (EXT // 2, EXT + 1)), one, 0)

    tot, more = box_sum(pay, sbuf, ssend.at[0], srecv.at[0], flip)
    sent += wcopies + more
    n_vox = tot[1:2, 0:1]
    s1, s2 = to_cols(tot[0:1, :])
    mean = s1 / n_vox
    var = s2 / n_vox - mean * mean
    inv = 1.0 / jnp.sqrt(var + 1e-05)
    gain, shift = to_col(gain_ref[...]), to_col(shift_ref[...])

    def fwd(j, carry):
        a, s = carry
        cols = pl.ds(pl.multiple_of(j * BLOCK, BLOCK), BLOCK)
        occ = occ_of(occ_ref, j)
        nd = (conv_ref[j] - mean) * inv
        sh = nd * gain + shift
        out_ref[:, cols] = (occ * jnp.maximum(sh, 0.0)).astype(BF16)
        rg = jnp.where(sh > 0.0, occ * grad_ref[:, cols].astype(F32), 0.0)
        prod[pl.ds(4 * j, 2)] = nd.reshape(2, HROWS, BLOCK)
        prod[pl.ds(4 * j + 2, 2)] = rg.reshape(2, HROWS, BLOCK)
        return a + rg, s + rg * nd

    zero = jnp.zeros((LOC, BLOCK), F32)
    a, s = lax.fori_loop(0, BLOCKS, fwd, (zero, zero))
    row = to_row(a, s)

    def turn(step):
        if step == 0:
            return
        for c in wcopies:
            c.wait_recv()
        for p in range(WPAD // BLOCK):
            win[pl.ds(p * BLOCK, BLOCK), :] = wrecv[:, pl.ds(p * BLOCK, BLOCK)].T

    tot, more = box_sum(row, sbuf2, ssend.at[1], srecv.at[1], turn)
    sent += more
    stat_ref[...] = tot
    sg, gg = to_cols(tot)
    scale = inv * gain
    sgm = sg / n_vox

    def bwd(j, _):
        nd = prod[pl.ds(4 * j, 2)].reshape(LOC, BLOCK)
        rg = prod[pl.ds(4 * j + 2, 2)].reshape(LOC, BLOCK)
        own[j] = (occ_of(occ_ref, j) * scale * (rg - sgm - nd * gg / n_vox)).astype(BF16)
        return 0

    lax.fori_loop(0, BLOCKS, bwd, 0)
    gather.start()

    def kterm(k, _):
        lhs = jnp.concatenate([own[j] for j in range(BLOCKS)], axis=1)
        rhs = jnp.concatenate([extt[map_ref[0, k, j]] for j in range(BLOCKS)], axis=0)
        wg[k] = jnp.dot(lhs, rhs, preferred_element_type=F32)
        return 0

    def send(src, dst, h, i, dev):
        c = rcopy(src, dst, gsend.at[h, i], grecv.at[h, i], dev)
        c.start()
        sent.append(c)
        return c

    flight = [None, None]
    xpart = lambda i: pl.ds(pl.multiple_of(i * XROWS, XROWS), XROWS)
    zpart = lambda i: pl.ds(pl.multiple_of(i * ZROWS, ZROWS), ZROWS)
    mine = pl.ds(pl.multiple_of(x * XROWS + z * ZROWS, ZROWS), ZROWS)

    def arrive(h):
        for c in flight[h]:
            c.wait_recv()

    def each_k(h, body):
        def one(k, _):
            body(k + h * KHALF, pl.ds(pl.multiple_of(k * LOC, LOC), LOC))
            return 0

        lax.fori_loop(0, KCOUNT[h], one, 0)

    def step0(h):
        def cut(k, rows):
            give[h, rows, :] = jnp.where(core == 0, wg[k, :, BLOCK:], wg[k, :, :BLOCK]).astype(BF16)

        each_k(h, cut)
        rows = pl.ds(0, KCOUNT[h] * LOC)
        flight[h] = [send(give.at[h, rows], given.at[h, rows], h, 0, mate)]

    def step1(h):
        arrive(h)

        def add(k, rows):
            keep = jnp.where(core == 0, wg[k, :, :BLOCK], wg[k, :, BLOCK:])
            xbuf[h, rows, :] = (keep + given[h, rows, :].astype(F32)).astype(BF16)

        each_k(h, add)
        rest = pl.ds(KCOUNT[h] * LOC, WROWS - KCOUNT[h] * LOC)
        xbuf[h, rest, :] = jnp.zeros((WROWS - KCOUNT[h] * LOC, BLOCK), BF16)
        flight[h] = [
            send(xbuf.at[h, xpart(lax.rem(x + d, 4))], xin.at[h, d - 1], h, d, xpeers[d - 1]) for d in range(1, 4)
        ]

    def step2(h):
        arrive(h)
        t = xbuf[h, xpart(x), :].astype(F32)
        for d in range(3):
            t = t + xin[h, d].astype(F32)
        zbuf[h] = t.astype(BF16)
        flight[h] = [
            send(zbuf.at[h, zpart(lax.rem(z + d, 8))], zin.at[h, d - 1], h, 3 + d, zpeers[d - 1]) for d in range(1, 8)
        ]

    def step3(h):
        arrive(h)
        t = zbuf[h, zpart(z), :].astype(F32)
        for d in range(7):
            t = t + zin[h, d].astype(F32)
        res[h, 0, mine, :] = t.astype(BF16)
        flight[h] = [
            send(res.at[h, 0, mine], res.at[h, 0, mine], h, 10 + d, zpeers[d - 1]) for d in range(1, 8)
        ]

    def step4(h):
        arrive(h)
        part = xpart(x)
        flight[h] = [
            send(res.at[h, 0, part], res.at[h, 0, part], h, 17 + d, xpeers[d - 1]) for d in range(1, 4)
        ]

    def step5(h):
        arrive(h)
        rows = pl.ds(0, KCOUNT[h] * LOC)
        flight[h] = [send(res.at[h, 0, rows], res.at[h, 1, rows], h, 21, mate)]

    def step6(h):
        arrive(h)

        def put(k, rows):
            m, o = res[h, 0, rows, :], res[h, 1, rows, :]
            wout_ref[k, :, :BLOCK] = jnp.where(core == 0, m, o)
            wout_ref[k, :, BLOCK:] = jnp.where(core == 0, o, m)

        each_k(h, put)

    lax.fori_loop(0, 8, kterm, 0)
    gather.forward(0)
    lax.fori_loop(8, KHALF, kterm, 0)
    step0(0)
    gather.forward(1)
    lax.fori_loop(KHALF, 19, kterm, 0)
    step1(0)
    lax.fori_loop(19, OFFSETS, kterm, 0)
    step0(1)
    gather.wait_part(0)
    gather.wait_part(1)
    step2(0)
    step1(1)

    def tile(t, _):
        halves = []
        for e in (2 * t, 2 * t + 1):
            halves.append(jnp.concatenate([own[e], from_dn[e], from_up[e], opp[e]], axis=0))
        rhs = jnp.concatenate(halves, axis=1)
        r = jnp.dot(win[pl.ds(0, OFFSETS * LOC), :], rhs, preferred_element_type=F32)
        place = 4 * OFFSETS * t
        prod[pl.ds(place, 2 * OFFSETS)] = r[:, :BLOCK].reshape(2 * OFFSETS, HROWS, BLOCK)
        prod[pl.ds(place + 2 * OFFSETS, 2 * OFFSETS)] = r[:, BLOCK:].reshape(2 * OFFSETS, HROWS, BLOCK)
        return 0

    lax.fori_loop(0, BLOCKS // 4, tile, 0)
    step2(1)
    lax.fori_loop(BLOCKS // 4, BLOCKS // 2, tile, 0)
    step3(0)

    fcopies = []
    for h in range(2):

        def walk(g, acc):
            for u in range(WALK):
                row, col = g // (BLOCK // WALK), lax.rem(g, BLOCK // WALK) * WALK + u
                acc = jnp.where(meta_ref[8 + row, col] > 0, 0.0, acc) + prod[meta_ref[row, col] + h]
                run[g * WALK + u] = acc
            return acc

        lax.fori_loop(0, OFFSETS * BLOCKS // WALK, walk, jnp.zeros((HROWS, BLOCK), F32))
        rows = pl.ds(h * HROWS, HROWS)

        def total(d):
            return jnp.where(meta_ref[15, d] > 0, run[meta_ref[7, d]], 0.0)

        for s in range(2 * SLOTS):
            fout[h, s // SLOTS, s % SLOTS] = total(BLOCKS + s).astype(BF16)
        for d, dev in enumerate((below, above)):
            c = rcopy(fout.at[h, d], fin.at[h, d], fsend.at[h, d], frecv.at[h, d], dev)
            c.start()
            fcopies.append(c)

        def keep(d, _):
            eg[d, rows, :] = total(d)
            return 0

        lax.fori_loop(0, BLOCKS, keep, 0)
        if h == 0:
            step3(1)
    step4(0)
    step4(1)
    for c in fcopies:
        c.wait_recv()
    sent += fcopies
    up_ok = b < NBOX - 1
    dn_ok = b > 0

    def settle(d, _):
        cols = pl.ds(pl.multiple_of(d * BLOCK, BLOCK), BLOCK)
        for h in range(2):
            rows = pl.ds(h * HROWS, HROWS)
            t = eg[d, rows, :]
            for s in range(SLOTS):
                t = t + jnp.where((send_ref[0, 1, s] == d) & up_ok, fin[h, 0, s].astype(F32), 0.0)
                t = t + jnp.where((send_ref[0, 0, s] == d) & dn_ok, fin[h, 1, s].astype(F32), 0.0)
            in_ref[rows, cols] = (occ_of(occ_ref, d) * t).astype(BF16)
        return 0

    lax.fori_loop(0, BLOCKS, settle, 0)
    step5(0)
    step5(1)
    step6(0)
    step6(1)
    gather.wait_sends()
    for c in sent:
        c.wait_send()


def norm_call(send, kmap, meta, conv, sums, out_grad, occ, gain, shift, ext, parts):
    quarter = pltpu.VMEM((BLOCKS, LOC, BLOCK), BF16)
    faces = pltpu.VMEM((2, 2, SLOTS, HROWS, BLOCK), BF16)
    dma = pltpu.SemaphoreType.DMA
    return pl.pallas_call(
        norm_kernel,
        out_shape=(
            jax.ShapeDtypeStruct((LOC, BLOCKS * BLOCK), BF16),
            jax.ShapeDtypeStruct((LOC, BLOCKS * BLOCK), BF16),
            jax.ShapeDtypeStruct((OFFSETS, LOC, CH), BF16),
            jax.ShapeDtypeStruct((1, BLOCK), F32),
        ),
        in_specs=[SMEM] * 3 + [VMEM] * 8,
        out_specs=(VMEM,) * 4,
        scratch_shapes=[
            pltpu.VMEM((EXT + 1, BLOCK, CH), BF16),
            pltpu.VMEM((OFFSETS, LOC, CH), F32),
            pltpu.VMEM((CH, WPAD), BF16),
            pltpu.VMEM((WPAD, CH), BF16),
            pltpu.VMEM((BLOCKS * 2 * OFFSETS, HROWS, BLOCK), F32),
            pltpu.VMEM((OFFSETS * BLOCKS, HROWS, BLOCK), F32),
            pltpu.VMEM((BLOCKS, LOC, BLOCK), F32),
            quarter,
            quarter,
            quarter,
            quarter,
            pltpu.VMEM((2, 8, 2, BLOCK), F32),
            pltpu.VMEM((2, 8, 1, BLOCK), F32),
            faces,
            faces,
            pltpu.VMEM((2, KHALF * LOC, BLOCK), BF16),
            pltpu.VMEM((2, KHALF * LOC, BLOCK), BF16),
            pltpu.VMEM((2, WROWS, BLOCK), BF16),
            pltpu.VMEM((2, 3, XROWS, BLOCK), BF16),
            pltpu.VMEM((2, XROWS, BLOCK), BF16),
            pltpu.VMEM((2, 7, ZROWS, BLOCK), BF16),
            pltpu.VMEM((2, 2, WROWS, BLOCK), BF16),
            dma((12,)),
            dma((12,)),
            dma((2, 2, 7)),
            dma((2, 2, 7)),
            dma((3,)),
            dma((3,)),
            dma((2, 2)),
            dma((2, 2)),
            dma((2, 22)),
            dma((2, 22)),
        ],
        compiler_params=params(2),
        name="norm",
    )(send, kmap, meta, conv, sums, out_grad, occ, gain, shift, ext, parts)


def per_device(
    features, occupied, send_lists, kernel_map, weights, norm_gain, norm_shift, out_grad
):
    occ = occupied.reshape(BLOCKS, 1, BLOCK)
    w = weights.reshape(OFFSETS * LOC, CH)
    gain, shift = norm_gain.reshape(1, LOC), norm_shift.reshape(1, LOC)
    conv, sums, ext, parts, meta = conv_call(send_lists, kernel_map, features, occ, w)
    out_features, in_grad, weight_grad, stat = norm_call(
        send_lists, kernel_map, meta, conv, sums, out_grad, occ, gain, shift, ext, parts
    )
    return (out_features, in_grad, weight_grad.astype(F32), stat[0, LOC:], stat[0, :LOC])


def solution(mesh):
    in_specs = (
        P("ch", "box"),
        P("box"),
        P("box", None, None),
        P("box", None, None),
        P(None, "ch", None),
        P("ch"),
        P("ch"),
        P("ch", "box"),
    )
    out_specs = (P("ch", "box"), P("ch", "box"), P(None, "ch", None), P("ch"), P("ch"))
    return jax.shard_map(
        per_device, mesh=mesh, in_specs=in_specs, out_specs=out_specs, check_vma=False
    )
```

time: 157 us -> 127 us (0.81)
  Pallas kernels: 145 us -> 118 us
  local copies, waits for them, and re-layouts: 7.16 us -> 5.25 us
    pallas_call x2 -> x0, Pallas kernels: 53.1 us -> none  [the longest x1 39.2 us: final_call(): pl.pallas_call(final_kernel, out_shape=(jax.ShapeDtypeStruct((LOC, BLOCKS...]
    pallas_call x1, Pallas kernels: 51.3 us -> 77.9 us  [norm_call(): pl.pallas_call(norm_kernel, out_shape=(jax.ShapeDtypeStruct((LOC, BLOCKS...]
    reshape x2 -> x0, local copies, waits for them, and re-layouts: 2.01 us -> none  [the longest x1 1.35 us: per_device(): send = send_lists.reshape(2 * SLOTS)]
    unnamed x7 -> x5, local copies, waits for them, and re-layouts: 3.88 us -> 3.98 us
where the time goes in v3:
time: 127 us
  Pallas kernels  118 us (93%)
  local copies, waits for them, and re-layouts  5.25 us (4%)
  other arithmetic  2.59 us (2%)
    pallas_call x1, Pallas kernels, norm_call(): pl.pallas_call(norm_kernel, out_shape=(jax.ShapeDtypeStruct((LOC, BLOCKS...  77.9 us
    pallas_call x1, Pallas kernels, conv_call(): pl.pallas_call(conv_kernel, out_shape=(jax.ShapeDtypeStruct((BLOCKS, LOC,...  40.5 us
    unnamed x5, local copies, waits for them, and re-layouts  3.98 us
    convert_element_type x1, other arithmetic, per_device(): weight_grad.astype(F32)  2.59 us

profile of v3, /device:TPU:1, one launch (start us, length us, event | category | flops | bytes accessed | tf_op | source)
XLA Modules:
  0.0 126.9 jit_solution(1069755716454362987)
XLA Ops:
  0.6 1.3 %copy.14.map_ref = s32[1,27,32]{2,1,0:T(8,128)} copy(s32[1,27,32]{2,0,1:T(1,128)} %param.11) | data formatting | bytes 6912 | tf_op args[3]
  1.9 40.5 %conv.1 = (f32[32,64,128]{2,1,0:T(8,128)}, f32[2,64,128]{2,1,0:T(8,128)}, bf16[49,256,128]{2,1,0:T(8,128)(2,1)}, bf16[4,64,1792]{2,1,0:T(8,128)(2,1)}, s32[16,128]{1,0:T(8,128)}) custom-call(s32[1,2,8]{2,1,0:T(2,128)} %send_ref.3, s32[1,27,32]{2,1,0:T(8,128)} %copy.14.map_ref, bf16[64,4096]{1,0:T(8,128)(2,1)} %feat_ref.1, s32[32,1,128]{2,1,0:T(1,128)} %bitcast.9, ...), custom_call_target="tpu_custom_call" | custom-call | tf_op jit(solution)/shard_map/conv/pallas_call | solution.py:287
  42.5 77.9 %norm.1 = (bf16[64,4096]{1,0:T(8,128)(2,1)}, bf16[64,4096]{1,0:T(8,128)(2,1)}, bf16[27,64,256]{2,1,0:T(8,128)(2,1)}, f32[1,128]{1,0:T(1,128)}) custom-call(s32[1,2,8]{2,1,0:T(2,128)} %send_ref.3, s32[1,27,32]{2,1,0:T(8,128)} %copy.14.map_ref, s32[16,128]{1,0:T(8,128)} %get-tuple-element.14.meta_ref, f32[32,64,128]{2,1,0:T(8,128)} %get-tuple-element.15.conv_ref, ...), custom_call_target="tpu_custom_call" | custom-call | tf_op jit(solution)/shard_map/norm/pallas_call | solution.py:691
  120.4 0.0 copy-start
  120.4 1.3 slice_bitcast_fusion
  121.7 2.6 %convert_element_type.3 = f32[27,64,256]{2,1,0:T(8,128)} convert(bf16[27,64,256]{2,1,0:T(8,128)(2,1)} %get-tuple-element.21) | non-fusion elementwise | flops 442368 | bytes 2654208 | tf_op jit(solution)/shard_map/convert_element_type | solution.py:750
  124.3 1.9 %copy.17 = bf16[64,4096]{1,0:T(8,128)(2,1)} copy(bf16[64,4096]{1,0:T(8,128)(2,1)} %get-tuple-element.30) | data formatting | bytes 1048576
  126.1 0.0 copy-done
  126.1 0.8 copy.18
Async XLA Ops:
  120.4 5.7 %copy-start = (bf16[64,4096]{1,0:T(8,128)(2,1)S(1)}, bf16[64,4096]{1,0:T(8,128)(2,1)}, u32[]{:S(2)}) copy-start(bf16[64,4096]{1,0:T(8,128)(2,1)} %get-tuple-element.31) | copy-start | bytes 1572868

commit v4 on v3

--- a/solution.py
+++ b/solution.py
@@ -23,13 +23,13 @@
 CH = 256
 LOC = 64
 WPAD = 1792
-KHALF = 14
-KCOUNT = (14, 13)
-WROWS = 1024
+PARTS = 4
+KFIRST = (0, 8, 16, 24)
+KCOUNT = (8, 8, 8, 3)
+WROWS = 512
 XROWS = WROWS // 4
 ZROWS = XROWS // 8
 NBOX = 64
-HROWS = 32
 WALK = 16
 
 
@@ -107,7 +107,7 @@
 
     def fill(k, target):
         for j in range(BLOCKS):
-            target = jnp.where(at == k * BLOCKS + j, map_ref[0, k, j], target)
+            target = jnp.where(at == k * BLOCKS + j, map_ref[k, 0, j], target)
         return target
 
     target = lax.fori_loop(0, OFFSETS, fill, jnp.full((8, BLOCK), 63, jnp.int32))
@@ -115,7 +115,7 @@
 
     def count(k, rank):
         for j in range(BLOCKS):
-            rank = rank + (keys > map_ref[0, k, j] * 1024 + (k * BLOCKS + j)).astype(jnp.int32)
+            rank = rank + (keys > map_ref[k, 0, j] * 1024 + (k * BLOCKS + j)).astype(jnp.int32)
         return rank
 
     return target, lax.fori_loop(0, OFFSETS, count, jnp.zeros((8, BLOCK), jnp.int32))
@@ -131,7 +131,7 @@
         rcol = jnp.broadcast_to(rank[s : s + 1, :].astype(F32), (BLOCK, BLOCK)).T
         tcol = jnp.broadcast_to(target[s : s + 1, :].astype(F32), (BLOCK, BLOCK)).T
         i = sub + s * BLOCK
-        number = (lax.rem(i, BLOCKS) * (2 * OFFSETS) + 2 * (i // BLOCKS)).astype(F32)
+        number = (lax.rem(i, BLOCKS) * OFFSETS + i // BLOCKS).astype(F32)
         for r in range(7):
             hit = rcol == (lane + r * BLOCK).astype(F32)
             pair[r] = pair[r] + jnp.sum(jnp.where(hit, number, 0.0), axis=0, keepdims=True)
@@ -216,7 +216,7 @@
             tile(t)
             return 0
 
-        lax.fori_loop(0, CHUNK, one, 0)
+        lax.fori_loop(0, CHUNK, one, 0, unroll=2)
 
     copies = [pack(0, own)]
     prod[EXT] = jnp.zeros((OFFSETS * LOC, BLOCK), F32)
@@ -234,9 +234,8 @@
             parts_ref[2 * h, :, put] = jnp.where(low, first, pltpu.roll(second, LOC, 1)).astype(BF16)
             parts_ref[2 * h + 1, :, put] = jnp.where(low, pltpu.roll(first, LOC, 1), second).astype(BF16)
     gather.forward(0)
-    ranks = rank_pairs(map_ref)
     gather.forward(1)
-    meta_ref[...] = sort_pairs(*ranks)
+    meta_ref[...] = sort_pairs(*rank_pairs(map_ref))
     gather.wait_part(0)
     part_tiles(0)
     gather.wait_part(1)
@@ -259,19 +258,19 @@
         tile(t)
         return 0
 
-    lax.fori_loop(BLOCKS // 2, EXT // 2, face_tile, 0)
+    lax.fori_loop(BLOCKS // 2, EXT // 2, face_tile, 0, unroll=2)
 
     def out(j, carry):
         a, s = carry
         acc = prod[map_ref[0, 0, j], pl.ds(0, LOC), :]
         for k in range(1, OFFSETS):
-            acc = acc + prod[map_ref[0, k, j], pl.ds(LOC * k, LOC), :]
+            acc = acc + prod[map_ref[k, 0, j], pl.ds(LOC * k, LOC), :]
         conv_ref[j] = acc
         o = occ_of(occ_ref, j) * acc
         return a + o, s + o * acc
 
     zero = jnp.zeros((LOC, BLOCK), F32)
-    a, s = lax.fori_loop(0, BLOCKS, out, (zero, zero))
+    a, s = lax.fori_loop(0, BLOCKS, out, (zero, zero), unroll=2)
     sum_ref[0] = a
     sum_ref[1] = s
     gather.wait_sends()
@@ -384,8 +383,9 @@
     ext_ref,
     parts_ref,
     out_ref,
-    in_ref,
-    wout_ref,
+    eg,
+    fin,
+    res,
     stat_ref,
     extt,
     wg,
@@ -393,7 +393,6 @@
     win,
     prod,
     run,
-    eg,
     own,
     from_dn,
     from_up,
@@ -401,14 +400,12 @@
     sbuf,
     sbuf2,
     fout,
-    fin,
     give,
     given,
     xbuf,
     xin,
     zbuf,
     zin,
-    res,
     ysend,
     yrecv,
     ssend,
@@ -471,23 +468,21 @@
         sh = nd * gain + shift
         out_ref[:, cols] = (occ * jnp.maximum(sh, 0.0)).astype(BF16)
         rg = jnp.where(sh > 0.0, occ * grad_ref[:, cols].astype(F32), 0.0)
-        prod[pl.ds(4 * j, 2)] = nd.reshape(2, HROWS, BLOCK)
-        prod[pl.ds(4 * j + 2, 2)] = rg.reshape(2, HROWS, BLOCK)
+        run[2 * j] = nd
+        run[2 * j + 1] = rg
         return a + rg, s + rg * nd
 
     zero = jnp.zeros((LOC, BLOCK), F32)
     a, s = lax.fori_loop(0, BLOCKS, fwd, (zero, zero))
     row = to_row(a, s)
 
-    def turn(step):
-        if step == 0:
-            return
+    def turn():
         for c in wcopies:
             c.wait_recv()
         for p in range(WPAD // BLOCK):
             win[pl.ds(p * BLOCK, BLOCK), :] = wrecv[:, pl.ds(p * BLOCK, BLOCK)].T
 
-    tot, more = box_sum(row, sbuf2, ssend.at[1], srecv.at[1], turn)
+    tot, more = box_sum(row, sbuf2, ssend.at[1], srecv.at[1], lambda step: None)
     sent += more
     stat_ref[...] = tot
     sg, gg = to_cols(tot)
@@ -495,8 +490,7 @@
     sgm = sg / n_vox
 
     def bwd(j, _):
-        nd = prod[pl.ds(4 * j, 2)].reshape(LOC, BLOCK)
-        rg = prod[pl.ds(4 * j + 2, 2)].reshape(LOC, BLOCK)
+        nd, rg = run[2 * j], run[2 * j + 1]
         own[j] = (occ_of(occ_ref, j) * scale * (rg - sgm - nd * gg / n_vox)).astype(BF16)
         return 0
 
@@ -505,7 +499,7 @@
 
     def kterm(k, _):
         lhs = jnp.concatenate([own[j] for j in range(BLOCKS)], axis=1)
-        rhs = jnp.concatenate([extt[map_ref[0, k, j]] for j in range(BLOCKS)], axis=0)
+        rhs = jnp.concatenate([extt[map_ref[k, 0, j]] for j in range(BLOCKS)], axis=0)
         wg[k] = jnp.dot(lhs, rhs, preferred_element_type=F32)
         return 0
 
@@ -515,7 +509,7 @@
         sent.append(c)
         return c
 
-    flight = [None, None]
+    flight = [None] * PARTS
     xpart = lambda i: pl.ds(pl.multiple_of(i * XROWS, XROWS), XROWS)
     zpart = lambda i: pl.ds(pl.multiple_of(i * ZROWS, ZROWS), ZROWS)
     mine = pl.ds(pl.multiple_of(x * XROWS + z * ZROWS, ZROWS), ZROWS)
@@ -526,7 +520,7 @@
 
     def each_k(h, body):
         def one(k, _):
-            body(k + h * KHALF, pl.ds(pl.multiple_of(k * LOC, LOC), LOC))
+            body(k + KFIRST[h], pl.ds(pl.multiple_of(k * LOC, LOC), LOC))
             return 0
 
         lax.fori_loop(0, KCOUNT[h], one, 0)
@@ -547,8 +541,9 @@
             xbuf[h, rows, :] = (keep + given[h, rows, :].astype(F32)).astype(BF16)
 
         each_k(h, add)
-        rest = pl.ds(KCOUNT[h] * LOC, WROWS - KCOUNT[h] * LOC)
-        xbuf[h, rest, :] = jnp.zeros((WROWS - KCOUNT[h] * LOC, BLOCK), BF16)
+        rest = WROWS - KCOUNT[h] * LOC
+        if rest:
+            xbuf[h, pl.ds(KCOUNT[h] * LOC, rest), :] = jnp.zeros((rest, BLOCK), BF16)
         flight[h] = [
             send(xbuf.at[h, xpart(lax.rem(x + d, 4))], xin.at[h, d - 1], h, d, xpeers[d - 1]) for d in range(1, 4)
         ]
@@ -585,29 +580,29 @@
         rows = pl.ds(0, KCOUNT[h] * LOC)
         flight[h] = [send(res.at[h, 0, rows], res.at[h, 1, rows], h, 21, mate)]
 
-    def step6(h):
-        arrive(h)
-
-        def put(k, rows):
-            m, o = res[h, 0, rows, :], res[h, 1, rows, :]
-            wout_ref[k, :, :BLOCK] = jnp.where(core == 0, m, o)
-            wout_ref[k, :, BLOCK:] = jnp.where(core == 0, o, m)
-
-        each_k(h, put)
-
-    lax.fori_loop(0, 8, kterm, 0)
+    def kterms(first, last):
+        lax.fori_loop(first, last, kterm, 0)
+
+    kterms(0, 8)
+    step0(0)
     gather.forward(0)
-    lax.fori_loop(8, KHALF, kterm, 0)
-    step0(0)
+    kterms(8, 12)
+    step1(0)
+    kterms(12, 16)
+    step0(1)
     gather.forward(1)
-    lax.fori_loop(KHALF, 19, kterm, 0)
-    step1(0)
-    lax.fori_loop(19, OFFSETS, kterm, 0)
-    step0(1)
-    gather.wait_part(0)
-    gather.wait_part(1)
+    kterms(16, 20)
     step2(0)
     step1(1)
+    kterms(20, 24)
+    step0(2)
+    kterms(24, 27)
+    step0(3)
+    step2(1)
+    step1(2)
+    turn()
+    step3(0)
+    step1(3)
 
     def tile(t, _):
         halves = []
@@ -615,70 +610,65 @@
             halves.append(jnp.concatenate([own[e], from_dn[e], from_up[e], opp[e]], axis=0))
         rhs = jnp.concatenate(halves, axis=1)
         r = jnp.dot(win[pl.ds(0, OFFSETS * LOC), :], rhs, preferred_element_type=F32)
-        place = 4 * OFFSETS * t
-        prod[pl.ds(place, 2 * OFFSETS)] = r[:, :BLOCK].reshape(2 * OFFSETS, HROWS, BLOCK)
-        prod[pl.ds(place + 2 * OFFSETS, 2 * OFFSETS)] = r[:, BLOCK:].reshape(2 * OFFSETS, HROWS, BLOCK)
+        r = r.astype(BF16)
+        place = 2 * OFFSETS * t
+        prod[pl.ds(place, OFFSETS)] = r[:, :BLOCK].reshape(OFFSETS, LOC, BLOCK)
+        prod[pl.ds(place + OFFSETS, OFFSETS)] = r[:, BLOCK:].reshape(OFFSETS, LOC, BLOCK)
         return 0
 
-    lax.fori_loop(0, BLOCKS // 4, tile, 0)
-    step2(1)
-    lax.fori_loop(BLOCKS // 4, BLOCKS // 2, tile, 0)
-    step3(0)
-
+    gather.wait_part(0)
+    lax.fori_loop(0, 4, tile, 0)
+    lax.fori_loop(8, 12, tile, 0)
+    step2(2)
+    step2(3)
+    gather.wait_part(1)
+    lax.fori_loop(4, 8, tile, 0)
+    step3(1)
+    lax.fori_loop(12, 16, tile, 0)
+    step4(0)
+
+    def walk(g, acc):
+        for u in range(WALK):
+            row, col = g // (BLOCK // WALK), lax.rem(g, BLOCK // WALK) * WALK + u
+            term = prod[meta_ref[row, col]].astype(F32)
+            acc = jnp.where(meta_ref[8 + row, col] > 0, 0.0, acc) + term
+            run[g * WALK + u] = acc
+        return acc
+
+    steps = OFFSETS * BLOCKS // WALK
+    acc = lax.fori_loop(0, steps // 2, walk, jnp.zeros((LOC, BLOCK), F32))
+    step3(2)
+    step3(3)
+    lax.fori_loop(steps // 2, steps, walk, acc)
+
+    def total(d):
+        return jnp.where(meta_ref[15, d] > 0, run[meta_ref[7, d]], 0.0)
+
+    for s in range(2 * SLOTS):
+        fout[s // SLOTS, s % SLOTS] = total(BLOCKS + s).astype(BF16)
     fcopies = []
-    for h in range(2):
-
-        def walk(g, acc):
-            for u in range(WALK):
-                row, col = g // (BLOCK // WALK), lax.rem(g, BLOCK // WALK) * WALK + u
-                acc = jnp.where(meta_ref[8 + row, col] > 0, 0.0, acc) + prod[meta_ref[row, col] + h]
-                run[g * WALK + u] = acc
-            return acc
-
-        lax.fori_loop(0, OFFSETS * BLOCKS // WALK, walk, jnp.zeros((HROWS, BLOCK), F32))
-        rows = pl.ds(h * HROWS, HROWS)
-
-        def total(d):
-            return jnp.where(meta_ref[15, d] > 0, run[meta_ref[7, d]], 0.0)
-
-        for s in range(2 * SLOTS):
-            fout[h, s // SLOTS, s % SLOTS] = total(BLOCKS + s).astype(BF16)
-        for d, dev in enumerate((below, above)):
-            c = rcopy(fout.at[h, d], fin.at[h, d], fsend.at[h, d], frecv.at[h, d], dev)
-            c.start()
-            fcopies.append(c)
-
-        def keep(d, _):
-            eg[d, rows, :] = total(d)
-            return 0
-
-        lax.fori_loop(0, BLOCKS, keep, 0)
-        if h == 0:
-            step3(1)
-    step4(0)
+    for d, dev in enumerate((below, above)):
+        c = rcopy(fout.at[d], fin.at[d], fsend.at[d], frecv.at[d], dev)
+        c.start()
+        fcopies.append(c)
+    sent += fcopies
     step4(1)
+    step5(0)
+
+    def keep(d, _):
+        eg[d] = total(d)
+        return 0
+
+    lax.fori_loop(0, BLOCKS, keep, 0)
+    step4(2)
+    step4(3)
+    step5(1)
     for c in fcopies:
         c.wait_recv()
-    sent += fcopies
-    up_ok = b < NBOX - 1
-    dn_ok = b > 0
-
-    def settle(d, _):
-        cols = pl.ds(pl.multiple_of(d * BLOCK, BLOCK), BLOCK)
-        for h in range(2):
-            rows = pl.ds(h * HROWS, HROWS)
-            t = eg[d, rows, :]
-            for s in range(SLOTS):
-                t = t + jnp.where((send_ref[0, 1, s] == d) & up_ok, fin[h, 0, s].astype(F32), 0.0)
-                t = t + jnp.where((send_ref[0, 0, s] == d) & dn_ok, fin[h, 1, s].astype(F32), 0.0)
-            in_ref[rows, cols] = (occ_of(occ_ref, d) * t).astype(BF16)
-        return 0
-
-    lax.fori_loop(0, BLOCKS, settle, 0)
-    step5(0)
-    step5(1)
-    step6(0)
-    step6(1)
+    step5(2)
+    step5(3)
+    for h in range(PARTS):
+        arrive(h)
     gather.wait_sends()
     for c in sent:
         c.wait_send()
@@ -686,55 +676,98 @@
 
 def norm_call(send, kmap, meta, conv, sums, out_grad, occ, gain, shift, ext, parts):
     quarter = pltpu.VMEM((BLOCKS, LOC, BLOCK), BF16)
-    faces = pltpu.VMEM((2, 2, SLOTS, HROWS, BLOCK), BF16)
     dma = pltpu.SemaphoreType.DMA
     return pl.pallas_call(
         norm_kernel,
         out_shape=(
             jax.ShapeDtypeStruct((LOC, BLOCKS * BLOCK), BF16),
-            jax.ShapeDtypeStruct((LOC, BLOCKS * BLOCK), BF16),
-            jax.ShapeDtypeStruct((OFFSETS, LOC, CH), BF16),
+            jax.ShapeDtypeStruct((BLOCKS, LOC, BLOCK), F32),
+            jax.ShapeDtypeStruct((2, SLOTS, LOC, BLOCK), BF16),
+            jax.ShapeDtypeStruct((PARTS, 2, WROWS, BLOCK), BF16),
             jax.ShapeDtypeStruct((1, BLOCK), F32),
         ),
         in_specs=[SMEM] * 3 + [VMEM] * 8,
-        out_specs=(VMEM,) * 4,
+        out_specs=(VMEM,) * 5,
         scratch_shapes=[
             pltpu.VMEM((EXT + 1, BLOCK, CH), BF16),
             pltpu.VMEM((OFFSETS, LOC, CH), F32),
             pltpu.VMEM((CH, WPAD), BF16),
             pltpu.VMEM((WPAD, CH), BF16),
-            pltpu.VMEM((BLOCKS * 2 * OFFSETS, HROWS, BLOCK), F32),
-            pltpu.VMEM((OFFSETS * BLOCKS, HROWS, BLOCK), F32),
-            pltpu.VMEM((BLOCKS, LOC, BLOCK), F32),
+            pltpu.VMEM((OFFSETS * BLOCKS, LOC, BLOCK), BF16),
+            pltpu.VMEM((OFFSETS * BLOCKS, LOC, BLOCK), F32),
             quarter,
             quarter,
             quarter,
             quarter,
             pltpu.VMEM((2, 8, 2, BLOCK), F32),
             pltpu.VMEM((2, 8, 1, BLOCK), F32),
-            faces,
-            faces,
-            pltpu.VMEM((2, KHALF * LOC, BLOCK), BF16),
-            pltpu.VMEM((2, KHALF * LOC, BLOCK), BF16),
-            pltpu.VMEM((2, WROWS, BLOCK), BF16),
-            pltpu.VMEM((2, 3, XROWS, BLOCK), BF16),
-            pltpu.VMEM((2, XROWS, BLOCK), BF16),
-            pltpu.VMEM((2, 7, ZROWS, BLOCK), BF16),
-            pltpu.VMEM((2, 2, WROWS, BLOCK), BF16),
+            pltpu.VMEM((2, SLOTS, LOC, BLOCK), BF16),
+            pltpu.VMEM((PARTS, WROWS, BLOCK), BF16),
+            pltpu.VMEM((PARTS, WROWS, BLOCK), BF16),
+            pltpu.VMEM((PARTS, WROWS, BLOCK), BF16),
+            pltpu.VMEM((PARTS, 3, XROWS, BLOCK), BF16),
+            pltpu.VMEM((PARTS, XROWS, BLOCK), BF16),
+            pltpu.VMEM((PARTS, 7, ZROWS, BLOCK), BF16),
             dma((12,)),
             dma((12,)),
             dma((2, 2, 7)),
             dma((2, 2, 7)),
             dma((3,)),
             dma((3,)),
-            dma((2, 2)),
-            dma((2, 2)),
-            dma((2, 22)),
-            dma((2, 22)),
+            dma((2,)),
+            dma((2,)),
+            dma((PARTS, 22)),
+            dma((PARTS, 22)),
         ],
         compiler_params=params(2),
         name="norm",
     )(send, kmap, meta, conv, sums, out_grad, occ, gain, shift, ext, parts)
+
+
+def emit_kernel(
+    send_ref, out_ref, eg_ref, fin_ref, res_ref, stat_ref, occ_ref, out_to, in_to, wg_to, gain_to, shift_to, acc
+):
+    out_to[...] = out_ref[...]
+    b = lax.axis_index("box")
+    core = lax.rem(b, 2)
+    for h in range(PARTS):
+
+        def put(k, _):
+            rows = pl.ds(pl.multiple_of(k * LOC, LOC), LOC)
+            m, o = res_ref[h, 0, rows, :].astype(F32), res_ref[h, 1, rows, :].astype(F32)
+            wg_to[k + KFIRST[h], :, :BLOCK] = jnp.where(core == 0, m, o)
+            wg_to[k + KFIRST[h], :, BLOCK:] = jnp.where(core == 0, o, m)
+            return 0
+
+        lax.fori_loop(0, KCOUNT[h], put, 0)
+    shift_to[...] = stat_ref[:, :LOC]
+    gain_to[...] = stat_ref[:, LOC:]
+    acc[pl.ds(0, BLOCKS)] = eg_ref[...]
+    acc[BLOCKS] = jnp.zeros((LOC, BLOCK), F32)
+    for d, ok in ((0, b < NBOX - 1), (1, b > 0)):
+        for s in range(SLOTS):
+            at = send_ref[0, 1 - d, s]
+            acc[at] = acc[at] + jnp.where(ok, fin_ref[d, s].astype(F32), 0.0)
+
+    def settle(d, _):
+        in_to[:, pl.ds(pl.multiple_of(d * BLOCK, BLOCK), BLOCK)] = (occ_of(occ_ref, d) * acc[d]).astype(BF16)
+        return 0
+
+    lax.fori_loop(0, BLOCKS, settle, 0)
+
+
+def emit_call(send, occ, out_features, eg, fin, res, stat):
+    whole = jax.ShapeDtypeStruct((LOC, BLOCKS * BLOCK), BF16)
+    line = jax.ShapeDtypeStruct((1, LOC), F32)
+    return pl.pallas_call(
+        emit_kernel,
+        out_shape=(whole, whole, jax.ShapeDtypeStruct((OFFSETS, LOC, CH), F32), line, line),
+        in_specs=[SMEM] + [VMEM] * 6,
+        out_specs=(VMEM,) * 5,
+        scratch_shapes=[pltpu.VMEM((BLOCKS + 1, LOC, BLOCK), F32)],
+        compiler_params=params(),
+        name="emit",
+    )(send, out_features, eg, fin, res, stat, occ)
 
 
 def per_device(
@@ -742,12 +775,12 @@
 ):
     occ = occupied.reshape(BLOCKS, 1, BLOCK)
     w = weights.reshape(OFFSETS * LOC, CH)
+    kernel_map = kernel_map.transpose(1, 0, 2)
     gain, shift = norm_gain.reshape(1, LOC), norm_shift.reshape(1, LOC)
     conv, sums, ext, parts, meta = conv_call(send_lists, kernel_map, features, occ, w)
-    out_features, in_grad, weight_grad, stat = norm_call(
-        send_lists, kernel_map, meta, conv, sums, out_grad, occ, gain, shift, ext, parts
-    )
-    return (out_features, in_grad, weight_grad.astype(F32), stat[0, LOC:], stat[0, :LOC])
+    results = norm_call(send_lists, kernel_map, meta, conv, sums, out_grad, occ, gain, shift, ext, parts)
+    out_features, in_grad, weight_grad, gain_grad, shift_grad = emit_call(send_lists, occ, *results)
+    return (out_features, in_grad, weight_grad, gain_grad.reshape(LOC), shift_grad.reshape(LOC))
 
 
 def solution(mesh):

time: 127 us -> 119 us (0.937)
  local copies, waits for them, and re-layouts: 5.25 us -> 0 us
  other arithmetic: 2.59 us -> 0 us
    pallas_call x0 -> x1, Pallas kernels: none -> 4.01 us  [emit_call(): pl.pallas_call(emit_kernel, out_shape=(whole, whole, jax.ShapeDtypeStruct...]
    unnamed x5 -> x0, local copies, waits for them, and re-layouts: 3.98 us -> none
    pallas_call x1, Pallas kernels: 77.9 us -> 74.2 us  [norm_call(): pl.pallas_call(norm_kernel, out_shape=(jax.ShapeDtypeStruct((LOC, BLOCKS...]
    convert_element_type x1 -> x0, other arithmetic: 2.59 us -> none  [per_device(): weight_grad.astype(F32)]
where the time goes in v4:
time: 119 us
  Pallas kernels  118 us (99%)
    pallas_call x1, Pallas kernels, norm_call(): pl.pallas_call(norm_kernel, out_shape=(jax.ShapeDtypeStruct((LOC, BLOCKS...  74.2 us
    pallas_call x1, Pallas kernels, conv_call(): pl.pallas_call(conv_kernel, out_shape=(jax.ShapeDtypeStruct((BLOCKS, LOC,...  39.8 us
    pallas_call x1, Pallas kernels, emit_call(): pl.pallas_call(emit_kernel, out_shape=(whole, whole, jax.ShapeDtypeStruct...  4.01 us

profile of v4, /device:TPU:1, one launch (start us, length us, event | category | flops | bytes accessed | tf_op | source)
XLA Modules:
  0.0 118.7 jit_solution(14070648804548910578)
XLA Ops:
  0.6 39.8 %conv.1 = (f32[32,64,128]{2,1,0:T(8,128)}, f32[2,64,128]{2,1,0:T(8,128)}, bf16[49,256,128]{2,1,0:T(8,128)(2,1)}, bf16[4,64,1792]{2,1,0:T(8,128)(2,1)}, s32[16,128]{1,0:T(8,128)}) custom-call(s32[1,2,8]{2,1,0:T(2,128)} %send_ref.5, s32[27,1,32]{2,1,0:T(1,128)} %bitcast.11, bf16[64,4096]{1,0:T(8,128)(2,1)} %feat_ref.1, s32[32,1,128]{2,1,0:T(1,128)} %bitcast.8, ...), custom_call_target="tpu_custom_call" | custom-call | tf_op jit(solution)/shard_map/conv/pallas_call | solution.py:286
  40.4 74.2 %norm.1 = (bf16[64,4096]{1,0:T(8,128)(2,1)}, f32[32,64,128]{2,1,0:T(8,128)}, bf16[2,8,64,128]{3,2,1,0:T(8,128)(2,1)}, bf16[4,2,512,128]{3,2,1,0:T(8,128)(2,1)}, f32[1,128]{1,0:T(1,128)}) custom-call(s32[1,2,8]{2,1,0:T(2,128)} %send_ref.5, s32[27,1,32]{2,1,0:T(1,128)} %bitcast.12, s32[16,128]{1,0:T(8,128)} %get-tuple-element.20.meta_ref, ...), custom_call_target="tpu_custom_call" | custom-call | tf_op jit(solution)/shard_map/norm/pallas_call | solution.py:680
  114.7 4.0 %emit.1 = (bf16[64,4096]{1,0:T(8,128)(2,1)}, bf16[64,4096]{1,0:T(8,128)(2,1)}, f32[27,64,256]{2,1,0:T(8,128)}, f32[1,64]{1,0:T(1,128)}, f32[1,64]{1,0:T(1,128)}) custom-call(s32[1,2,8]{2,1,0:T(2,128)} %send_ref.5, bf16[64,4096]{1,0:T(8,128)(2,1)} %get-tuple-element.25.out_ref, f32[32,64,128]{2,1,0:T(8,128)} %get-tuple-element.26.eg_ref, ...), custom_call_target="tpu_custom_call" | custom-call | tf_op jit(solution)/shard_map/emit/pallas_call | solution.py:762

commit v5 on v4

--- a/solution.py
+++ b/solution.py
@@ -12,11 +12,14 @@
 MESH = pl.DeviceIdType.MESH
 VMEM = pl.BlockSpec(memory_space=pltpu.VMEM)
 SMEM = pl.BlockSpec(memory_space=pltpu.SMEM)
+ANY = pl.BlockSpec(memory_space=pl.ANY)
 VMEM_LIMIT = 62 * 2**20
 
 BLOCK = 128
 BLOCKS = 32
-CHUNK = 8
+CHUNK = 4
+NCHUNK = 8
+NFWD = 4
 SLOTS = 8
 EXT = BLOCKS + 2 * SLOTS
 OFFSETS = 27
@@ -72,27 +75,30 @@
             part = pl.ds(chunk * CHUNK, CHUNK)
             return rcopy(src.at[part], dst.at[part], ssem.at[i], rsem.at[i], dev)
 
-        self.own_up = [mk(own, from_dn, c, c, self.up) for c in range(4)]
-        self.own_dn = [mk(own, from_up, c, 4 + c, self.dn) for c in range(4)]
-        self.far_up = [mk(from_dn, opp, c, 8 + c, self.up) for c in (0, 1)]
-        self.far_dn = [mk(from_up, opp, c, 8 + c, self.dn) for c in (2, 3)]
+        lower, upper = range(NFWD), range(NFWD, NCHUNK)
+        self.own_up = [mk(own, from_dn, c, c, self.up) for c in range(NCHUNK)]
+        self.own_dn = [mk(own, from_up, c, NCHUNK + c, self.dn) for c in range(NCHUNK)]
+        self.far_up = [mk(from_dn, opp, c, 2 * NCHUNK + c, self.up) for c in lower]
+        self.far_dn = [mk(from_up, opp, c, 2 * NCHUNK + c, self.dn) for c in upper]
 
     def start(self):
-        self.own_up[0].start()
-        self.own_dn[2].start()
-        self.own_up[1].start()
-        self.own_dn[3].start()
+        for c in range(2):
+            self.own_up[c].start()
+            self.own_dn[NFWD + c].start()
 
     def forward(self, i):
         self.own_up[i].wait_recv()
         self.far_up[i].start()
-        self.own_up[2 + i].start()
-        self.own_dn[2 + i].wait_recv()
+        self.own_up[NFWD + i].start()
+        self.own_dn[NFWD + i].wait_recv()
         self.far_dn[i].start()
         self.own_dn[i].start()
+        if i + 2 < NFWD:
+            self.own_up[i + 2].start()
+            self.own_dn[NFWD + i + 2].start()
 
     def wait_part(self, i):
-        self.own_up[2 + i].wait_recv()
+        self.own_up[NFWD + i].wait_recv()
         self.own_dn[i].wait_recv()
         self.far_up[i].wait_recv()
         self.far_dn[i].wait_recv()
@@ -102,23 +108,30 @@
             c.wait_send()
 
 
-def rank_pairs(map_ref):
-    at = lax.broadcasted_iota(jnp.int32, (8, BLOCK), 0) * BLOCK + lax.broadcasted_iota(jnp.int32, (8, BLOCK), 1)
+def pair_places():
+    return lax.broadcasted_iota(jnp.int32, (8, BLOCK), 0) * BLOCK + lax.broadcasted_iota(jnp.int32, (8, BLOCK), 1)
+
+
+def pair_targets(map_ref):
+    at = pair_places()
 
     def fill(k, target):
         for j in range(BLOCKS):
             target = jnp.where(at == k * BLOCKS + j, map_ref[k, 0, j], target)
         return target
 
-    target = lax.fori_loop(0, OFFSETS, fill, jnp.full((8, BLOCK), 63, jnp.int32))
-    keys = target * 1024 + at
+    return lax.fori_loop(0, OFFSETS, fill, jnp.full((8, BLOCK), 63, jnp.int32))
+
+
+def pair_ranks(map_ref, target):
+    keys = target * 1024 + pair_places()
 
     def count(k, rank):
         for j in range(BLOCKS):
             rank = rank + (keys > map_ref[k, 0, j] * 1024 + (k * BLOCKS + j)).astype(jnp.int32)
         return rank
 
-    return target, lax.fori_loop(0, OFFSETS, count, jnp.zeros((8, BLOCK), jnp.int32))
+    return lax.fori_loop(0, OFFSETS, count, jnp.zeros((8, BLOCK), jnp.int32))
 
 
 def sort_pairs(target, rank):
@@ -157,9 +170,10 @@
     w_ref,
     conv_ref,
     sum_ref,
-    ext,
+    ext_to,
     parts_ref,
     meta_ref,
+    ext,
     own,
     from_dn,
     from_up,
@@ -171,6 +185,7 @@
     yrecv,
     fsend,
     frecv,
+    esem,
 ):
     q = lax.axis_index("ch")
     b = lax.axis_index("box")
@@ -208,7 +223,7 @@
 
     def part_tiles(i):
         def one(t, _):
-            t = t + i * (CHUNK // 2) + (t // (CHUNK // 2)) * (CHUNK // 2)
+            t = t + i * (CHUNK // 2) + (t // (CHUNK // 2)) * (3 * CHUNK // 2)
             for r_abs, src in quarters:
                 rows = rows_of(r_abs)
                 ext[2 * t, rows, :] = src[2 * t]
@@ -234,15 +249,20 @@
             parts_ref[2 * h, :, put] = jnp.where(low, first, pltpu.roll(second, LOC, 1)).astype(BF16)
             parts_ref[2 * h + 1, :, put] = jnp.where(low, pltpu.roll(first, LOC, 1), second).astype(BF16)
     gather.forward(0)
+    target = pair_targets(map_ref)
     gather.forward(1)
-    meta_ref[...] = sort_pairs(*rank_pairs(map_ref))
-    gather.wait_part(0)
-    part_tiles(0)
-    gather.wait_part(1)
+    rank = pair_ranks(map_ref, target)
+    gather.forward(2)
+    meta_ref[...] = sort_pairs(target, rank)
+    gather.forward(3)
+    for i in range(NFWD - 1):
+        gather.wait_part(i)
+        part_tiles(i)
+    gather.wait_part(NFWD - 1)
     copies.append(pack(1, from_dn))
     copies.append(pack(2, from_up))
     copies.append(pack(3, opp))
-    part_tiles(1)
+    part_tiles(NFWD - 1)
     keep_below = jnp.where(b > 0, 1.0, 0.0)
     keep_above = jnp.where(b < NBOX - 1, 1.0, 0.0)
     for r, (r_abs, _) in enumerate(quarters):
@@ -260,6 +280,9 @@
 
     lax.fori_loop(BLOCKS // 2, EXT // 2, face_tile, 0, unroll=2)
 
+    leave = pltpu.make_async_copy(ext, ext_to, esem)
+    leave.start()
+
     def out(j, carry):
         a, s = carry
         acc = prod[map_ref[0, 0, j], pl.ds(0, LOC), :]
@@ -273,6 +296,7 @@
     a, s = lax.fori_loop(0, BLOCKS, out, (zero, zero), unroll=2)
     sum_ref[0] = a
     sum_ref[1] = s
+    leave.wait()
     gather.wait_sends()
     for up, dn in copies:
         up.wait_send()
@@ -293,8 +317,9 @@
             jax.ShapeDtypeStruct((16, BLOCK), jnp.int32),
         ),
         in_specs=[SMEM, SMEM, VMEM, VMEM, VMEM],
-        out_specs=(VMEM,) * 5,
+        out_specs=(VMEM, VMEM, ANY, VMEM, VMEM),
         scratch_shapes=[
+            pltpu.VMEM((EXT + 1, CH, BLOCK), BF16),
             quarter,
             quarter,
             quarter,
@@ -302,10 +327,11 @@
             faces,
             faces,
             pltpu.VMEM((EXT + 1, OFFSETS * LOC, BLOCK), F32),
-            dma((12,)),
-            dma((12,)),
+            dma((3 * NCHUNK,)),
+            dma((3 * NCHUNK,)),
             dma((4, 2)),
             dma((4, 2)),
+            dma,
         ],
         compiler_params=params(1),
         name="conv",
@@ -376,17 +402,20 @@
     meta_ref,
     conv_ref,
     sum_ref,
-    grad_ref,
+    grad_from,
     occ_ref,
     gain_ref,
     shift_ref,
-    ext_ref,
+    ext_from,
     parts_ref,
     out_ref,
     eg,
     fin,
     res,
     stat_ref,
+    grad_ref,
+    ext_ref,
+    relay,
     extt,
     wg,
     wrecv,
@@ -416,35 +445,61 @@
     frecv,
     gsend,
     grecv,
+    lsem,
 ):
     q = lax.axis_index("ch")
     b = lax.axis_index("box")
     x, z, core = b // 16, lax.rem(b // 2, 8), lax.rem(b, 2)
     gather = YGather(own, from_dn, from_up, opp, ysend, yrecv)
     (_, near), (_, far) = box_groups()
-    ypeers = [{"ch": lax.rem(q + d, 4)} for d in range(1, 4)]
     above = {"box": lax.rem(b + 1, NBOX)}
     below = {"box": lax.rem(b + NBOX - 1, NBOX)}
     mate = at_box(x, z, 1 - core)
     xpeers = [at_box(lax.rem(x + d, 4), z, core) for d in range(1, 4)]
     zpeers = far
     sent = []
+    loads = [pltpu.make_async_copy(ext_from, ext_ref, lsem.at[0]), pltpu.make_async_copy(grad_from, grad_ref, lsem.at[1])]
+    for c in loads:
+        c.start()
 
     count = jnp.sum(occ_ref[...].astype(F32), axis=0)
     count = jnp.broadcast_to(jnp.sum(count, axis=1, keepdims=True), (1, BLOCK))
     row = to_row(sum_ref[0], sum_ref[1])
     sub = lax.broadcasted_iota(jnp.int32, (2, BLOCK), 0)
     pay = jnp.where(sub == 0, row, count)
-    greet(ypeers + near + far + [above, below])
+    greet([gather.up, gather.dn] + near + far + [above, below])
     wcopies = []
-    for d, slot in ((1, 1), (3, 2), (2, 3)):
-        dst = wrecv.at[pl.ds(slot * LOC, LOC)]
-        c = rcopy(parts_ref.at[lax.rem(q + d, 4)], dst, wsend.at[d - 1], wrecvs.at[d - 1], ypeers[d - 1])
+
+    def wcopy(src, dst, i, dev):
+        c = rcopy(src, dst, wsend.at[i], wrecvs.at[i], dev)
+        wcopies.append(c)
+        return c
+
+    far_part = parts_ref.at[lax.rem(q + 2, 4)]
+    near_rows, far_rows = pl.ds(0, LOC // 2), pl.ds(LOC // 2, LOC // 2)
+    lead = [
+        wcopy(far_part.at[near_rows], relay.at[0], 0, gather.up),
+        wcopy(far_part.at[far_rows], relay.at[1], 1, gather.dn),
+    ]
+    tail = [
+        wcopy(parts_ref.at[lax.rem(q + 1, 4)], wrecv.at[pl.ds(LOC, LOC)], 2, gather.up),
+        wcopy(parts_ref.at[lax.rem(q + 3, 4)], wrecv.at[pl.ds(2 * LOC, LOC)], 3, gather.dn),
+    ]
+    tail_far = [
+        wcopy(relay.at[0], wrecv.at[pl.ds(3 * LOC, LOC // 2)], 4, gather.up),
+        wcopy(relay.at[1], wrecv.at[pl.ds(3 * LOC + LOC // 2, LOC // 2)], 5, gather.dn),
+    ]
+    for c in lead + tail:
         c.start()
-        wcopies.append(c)
     wrecv[pl.ds(0, LOC), :] = parts_ref[q]
+    loads[0].wait()
 
     def flip(step):
+        if step == 1:
+            for c, d in zip(lead, tail_far):
+                c.wait_recv()
+                d.start()
+
         def one(e, _):
             extt[e] = ext_ref[e].T
             return 0
@@ -453,6 +508,7 @@
 
     tot, more = box_sum(pay, sbuf, ssend.at[0], srecv.at[0], flip)
     sent += wcopies + more
+    loads[1].wait()
     n_vox = tot[1:2, 0:1]
     s1, s2 = to_cols(tot[0:1, :])
     mean = s1 / n_vox
@@ -476,13 +532,15 @@
     a, s = lax.fori_loop(0, BLOCKS, fwd, (zero, zero))
     row = to_row(a, s)
 
-    def turn():
-        for c in wcopies:
+    def turn(step):
+        if step == 0:
+            return
+        for c in tail + tail_far:
             c.wait_recv()
         for p in range(WPAD // BLOCK):
             win[pl.ds(p * BLOCK, BLOCK), :] = wrecv[:, pl.ds(p * BLOCK, BLOCK)].T
 
-    tot, more = box_sum(row, sbuf2, ssend.at[1], srecv.at[1], lambda step: None)
+    tot, more = box_sum(row, sbuf2, ssend.at[1], srecv.at[1], turn)
     sent += more
     stat_ref[...] = tot
     sg, gg = to_cols(tot)
@@ -588,21 +646,22 @@
     gather.forward(0)
     kterms(8, 12)
     step1(0)
-    kterms(12, 16)
+    kterms(12, 14)
+    gather.forward(1)
+    kterms(14, 16)
     step0(1)
-    gather.forward(1)
     kterms(16, 20)
+    gather.forward(2)
     step2(0)
     step1(1)
     kterms(20, 24)
     step0(2)
-    kterms(24, 27)
+    kterms(24, 25)
+    gather.forward(3)
+    kterms(25, 27)
     step0(3)
     step2(1)
     step1(2)
-    turn()
-    step3(0)
-    step1(3)
 
     def tile(t, _):
         halves = []
@@ -616,15 +675,20 @@
         prod[pl.ds(place + OFFSETS, OFFSETS)] = r[:, BLOCK:].reshape(OFFSETS, LOC, BLOCK)
         return 0
 
-    gather.wait_part(0)
-    lax.fori_loop(0, 4, tile, 0)
-    lax.fori_loop(8, 12, tile, 0)
+    def tiles(i):
+        gather.wait_part(i)
+        lax.fori_loop(2 * i, 2 * i + 2, tile, 0)
+        lax.fori_loop(2 * i + 8, 2 * i + 10, tile, 0)
+
+    tiles(0)
+    step1(3)
+    step3(0)
+    tiles(1)
     step2(2)
+    tiles(2)
     step2(3)
-    gather.wait_part(1)
-    lax.fori_loop(4, 8, tile, 0)
     step3(1)
-    lax.fori_loop(12, 16, tile, 0)
+    tiles(3)
     step4(0)
 
     def walk(g, acc):
@@ -635,11 +699,14 @@
             run[g * WALK + u] = acc
         return acc
 
-    steps = OFFSETS * BLOCKS // WALK
-    acc = lax.fori_loop(0, steps // 2, walk, jnp.zeros((LOC, BLOCK), F32))
+    third = OFFSETS * BLOCKS // WALK // 3
+    acc = lax.fori_loop(0, third, walk, jnp.zeros((LOC, BLOCK), F32))
     step3(2)
+    acc = lax.fori_loop(third, 2 * third, walk, acc)
     step3(3)
-    lax.fori_loop(steps // 2, steps, walk, acc)
+    step4(1)
+    lax.fori_loop(2 * third, 3 * third, walk, acc)
+    step5(0)
 
     def total(d):
         return jnp.where(meta_ref[15, d] > 0, run[meta_ref[7, d]], 0.0)
@@ -652,8 +719,6 @@
         c.start()
         fcopies.append(c)
     sent += fcopies
-    step4(1)
-    step5(0)
 
     def keep(d, _):
         eg[d] = total(d)
@@ -686,9 +751,12 @@
             jax.ShapeDtypeStruct((PARTS, 2, WROWS, BLOCK), BF16),
             jax.ShapeDtypeStruct((1, BLOCK), F32),
         ),
-        in_specs=[SMEM] * 3 + [VMEM] * 8,
+        in_specs=[SMEM] * 3 + [VMEM, VMEM, ANY, VMEM, VMEM, VMEM, ANY, VMEM],
         out_specs=(VMEM,) * 5,
         scratch_shapes=[
+            pltpu.VMEM((LOC, BLOCKS * BLOCK), BF16),
+            pltpu.VMEM((EXT + 1, CH, BLOCK), BF16),
+            pltpu.VMEM((2, LOC // 2, WPAD), BF16),
             pltpu.VMEM((EXT + 1, BLOCK, CH), BF16),
             pltpu.VMEM((OFFSETS, LOC, CH), F32),
             pltpu.VMEM((CH, WPAD), BF16),
@@ -708,16 +776,17 @@
             pltpu.VMEM((PARTS, 3, XROWS, BLOCK), BF16),
             pltpu.VMEM((PARTS, XROWS, BLOCK), BF16),
             pltpu.VMEM((PARTS, 7, ZROWS, BLOCK), BF16),
-            dma((12,)),
-            dma((12,)),
+            dma((3 * NCHUNK,)),
+            dma((3 * NCHUNK,)),
             dma((2, 2, 7)),
             dma((2, 2, 7)),
-            dma((3,)),
-            dma((3,)),
+            dma((6,)),
+            dma((6,)),
             dma((2,)),
             dma((2,)),
             dma((PARTS, 22)),
             dma((PARTS, 22)),
+            dma((2,)),
         ],
         compiler_params=params(2),
         name="norm",

time: 119 us -> 115 us (0.966)
  Pallas kernels: 118 us -> 115 us
    pallas_call x1, Pallas kernels: 74.2 us -> 70.6 us  [norm_call(): pl.pallas_call(norm_kernel, out_shape=(jax.ShapeDtypeStruct((LOC, BLOCKS...]
where the time goes in v5:
time: 115 us
  Pallas kernels  115 us (100%)
    pallas_call x1, Pallas kernels, norm_call(): pl.pallas_call(norm_kernel, out_shape=(jax.ShapeDtypeStruct((LOC, BLOCKS...  70.6 us
    pallas_call x1, Pallas kernels, conv_call(): pl.pallas_call(conv_kernel, out_shape=(jax.ShapeDtypeStruct((BLOCKS, LOC,...  40 us
    pallas_call x1, Pallas kernels, emit_call(): pl.pallas_call(emit_kernel, out_shape=(whole, whole, jax.ShapeDtypeStruct...  4.01 us

profile of v5, /device:TPU:1, one launch (start us, length us, event | category | flops | bytes accessed | tf_op | source)
XLA Modules:
  0.0 115.2 jit_solution(12452253328472770908)
XLA Ops:
  0.6 40.0 %conv.1 = (f32[32,64,128]{2,1,0:T(8,128)}, f32[2,64,128]{2,1,0:T(8,128)}, bf16[49,256,128]{2,1,0:T(8,128)(2,1)}, bf16[4,64,1792]{2,1,0:T(8,128)(2,1)}, s32[16,128]{1,0:T(8,128)}) custom-call(s32[1,2,8]{2,1,0:T(2,128)} %send_ref.5, s32[27,1,32]{2,1,0:T(1,128)} %bitcast.11, bf16[64,4096]{1,0:T(8,128)(2,1)} %feat_ref.1, s32[32,1,128]{2,1,0:T(1,128)} %bitcast.8, ...), custom_call_target="tpu_custom_call" | custom-call | tf_op jit(solution)/shard_map/conv/pallas_call | solution.py:310
  40.6 70.6 %norm.1 = (bf16[64,4096]{1,0:T(8,128)(2,1)}, f32[32,64,128]{2,1,0:T(8,128)}, bf16[2,8,64,128]{3,2,1,0:T(8,128)(2,1)}, bf16[4,2,512,128]{3,2,1,0:T(8,128)(2,1)}, f32[1,128]{1,0:T(1,128)}) custom-call(s32[1,2,8]{2,1,0:T(2,128)} %send_ref.5, s32[27,1,32]{2,1,0:T(1,128)} %bitcast.12, s32[16,128]{1,0:T(8,128)} %get-tuple-element.20.meta_ref, ...), custom_call_target="tpu_custom_call" | custom-call | tf_op jit(solution)/shard_map/norm/pallas_call | solution.py:745
  111.2 4.0 %emit.1 = (bf16[64,4096]{1,0:T(8,128)(2,1)}, bf16[64,4096]{1,0:T(8,128)(2,1)}, f32[27,64,256]{2,1,0:T(8,128)}, f32[1,64]{1,0:T(1,128)}, f32[1,64]{1,0:T(1,128)}) custom-call(s32[1,2,8]{2,1,0:T(2,128)} %send_ref.5, bf16[64,4096]{1,0:T(8,128)(2,1)} %get-tuple-element.25.out_ref, f32[32,64,128]{2,1,0:T(8,128)} %get-tuple-element.26.eg_ref, ...), custom_call_target="tpu_custom_call" | custom-call | tf_op jit(solution)/shard_map/emit/pallas_call | solution.py:831

commit v6 on v5

--- a/solution.py
+++ b/solution.py
@@ -70,42 +70,79 @@
         q = lax.axis_index("ch")
         self.up = {"ch": lax.rem(q + 1, 4)}
         self.dn = {"ch": lax.rem(q + 3, 4)}
-
-        def mk(src, dst, chunk, i, dev):
-            part = pl.ds(chunk * CHUNK, CHUNK)
-            return rcopy(src.at[part], dst.at[part], ssem.at[i], rsem.at[i], dev)
-
-        lower, upper = range(NFWD), range(NFWD, NCHUNK)
-        self.own_up = [mk(own, from_dn, c, c, self.up) for c in range(NCHUNK)]
-        self.own_dn = [mk(own, from_up, c, NCHUNK + c, self.dn) for c in range(NCHUNK)]
-        self.far_up = [mk(from_dn, opp, c, 2 * NCHUNK + c, self.up) for c in lower]
-        self.far_dn = [mk(from_up, opp, c, 2 * NCHUNK + c, self.dn) for c in upper]
+        self.refs = own, from_dn, from_up, opp
+        self.sems = ssem, rsem
+
+    def copy(self, src, dst, chunk, i, dev):
+        part = pl.ds(chunk * CHUNK, CHUNK)
+        return rcopy(src.at[part], dst.at[part], self.sems[0].at[i], self.sems[1].at[i], dev)
+
+    def own_up(self, c):
+        return self.copy(self.refs[0], self.refs[1], c, c, self.up)
+
+    def own_dn(self, c):
+        return self.copy(self.refs[0], self.refs[2], c, NCHUNK + c, self.dn)
+
+    def far_up(self, c):
+        return self.copy(self.refs[1], self.refs[3], c, 2 * NCHUNK + c, self.up)
+
+    def far_dn(self, c):
+        return self.copy(self.refs[2], self.refs[3], c, 2 * NCHUNK + c, self.dn)
 
     def start(self):
         for c in range(2):
-            self.own_up[c].start()
-            self.own_dn[NFWD + c].start()
+            self.own_up(c).start()
+            self.own_dn(NFWD + c).start()
+
+    def start_near(self):
+        for c in range(NFWD):
+            self.own_up(c).start()
+            self.own_dn(NFWD + c).start()
+
+    def advance(self, i):
+        self.own_up(i).wait_recv()
+        self.own_up(NFWD + i).start()
+        self.own_dn(NFWD + i).wait_recv()
+        self.own_dn(i).start()
+
+    def start_far(self):
+        for c in range(NFWD):
+            self.far_up(c).start()
+            self.far_dn(NFWD + c).start()
+
+    def wait_near(self):
+        for c in range(NFWD):
+            self.own_up(NFWD + c).wait_recv()
+            self.own_dn(c).wait_recv()
+
+    def wait_far(self, i):
+        self.far_up(i).wait_recv()
+        self.far_dn(NFWD + i).wait_recv()
 
     def forward(self, i):
-        self.own_up[i].wait_recv()
-        self.far_up[i].start()
-        self.own_up[NFWD + i].start()
-        self.own_dn[NFWD + i].wait_recv()
-        self.far_dn[i].start()
-        self.own_dn[i].start()
+        self.own_up(i).wait_recv()
+        self.far_up(i).start()
+        self.own_up(NFWD + i).start()
+        self.own_dn(NFWD + i).wait_recv()
+        self.far_dn(NFWD + i).start()
+        self.own_dn(i).start()
         if i + 2 < NFWD:
-            self.own_up[i + 2].start()
-            self.own_dn[NFWD + i + 2].start()
+            self.own_up(i + 2).start()
+            self.own_dn(NFWD + i + 2).start()
 
     def wait_part(self, i):
-        self.own_up[NFWD + i].wait_recv()
-        self.own_dn[i].wait_recv()
-        self.far_up[i].wait_recv()
-        self.far_dn[i].wait_recv()
+        self.own_up(NFWD + i).wait_recv()
+        self.own_dn(i).wait_recv()
+        self.far_up(i).wait_recv()
+        self.far_dn(NFWD + i).wait_recv()
 
     def wait_sends(self):
-        for c in self.own_up + self.own_dn + self.far_up + self.far_dn:
-            c.wait_send()
+        for c in range(NCHUNK):
+            self.own_up(c).wait_send()
+            self.own_dn(c).wait_send()
+        for c in range(NFWD):
+            self.far_up(c).wait_send()
+            self.far_dn(NFWD + c).wait_send()
 
 
 def pair_places():
@@ -201,7 +238,7 @@
 
     lax.fori_loop(0, BLOCKS, mask, 0)
     greet([gather.up, gather.dn, above, below])
-    gather.start()
+    gather.start_near()
 
     def pack(r, src):
         for d in range(2):
@@ -209,11 +246,14 @@
                 pick = send_ref[0, d, s]
                 blk = src[jnp.minimum(pick, BLOCKS - 1)].astype(F32)
                 fout[r, d, s] = jnp.where(pick < BLOCKS, blk, 0.0).astype(BF16)
-        up = rcopy(fout.at[r, 1], fin.at[r, 0], fsend.at[r, 1], frecv.at[r, 0], above)
-        dn = rcopy(fout.at[r, 0], fin.at[r, 1], fsend.at[r, 0], frecv.at[r, 1], below)
-        up.start()
-        dn.start()
-        return up, dn
+        for c in face_copies(r):
+            c.start()
+
+    def face_copies(r):
+        return (
+            rcopy(fout.at[r, 1], fin.at[r, 0], fsend.at[r, 1], frecv.at[r, 0], above),
+            rcopy(fout.at[r, 0], fin.at[r, 1], fsend.at[r, 0], frecv.at[r, 1], below),
+        )
 
     def tile(t):
         rhs = jnp.concatenate([ext[2 * t], ext[2 * t + 1]], axis=1)
@@ -221,65 +261,72 @@
         prod[2 * t] = res[:, :BLOCK]
         prod[2 * t + 1] = res[:, BLOCK:]
 
-    def part_tiles(i):
-        def one(t, _):
-            t = t + i * (CHUNK // 2) + (t // (CHUNK // 2)) * (3 * CHUNK // 2)
+    def face_rows():
+        keep = jnp.where(b > 0, 1.0, 0.0), jnp.where(b < NBOX - 1, 1.0, 0.0)
+        for r, (r_abs, _) in enumerate(quarters):
+            for c in face_copies(r):
+                c.wait_recv()
+            rows = rows_of(r_abs)
+            for d in range(2):
+                for s in range(SLOTS):
+                    ext[BLOCKS + d * SLOTS + s, rows, :] = (fin[r, d, s].astype(F32) * keep[d]).astype(BF16)
+
+    def two_tiles(p, _):
+        first = jnp.where(p < NCHUNK, 2 * (p // 2) + NCHUNK * lax.rem(p, 2), 2 * p)
+
+        @pl.when((p < NCHUNK) & (lax.rem(p, 2) == 0))
+        def _():
+            gather.wait_far(p // 2)
+
+        @pl.when(p == NCHUNK - 2)
+        def _():
+            pack(3, opp)
+
+        @pl.when(p < NCHUNK)
+        def _():
             for r_abs, src in quarters:
                 rows = rows_of(r_abs)
-                ext[2 * t, rows, :] = src[2 * t]
-                ext[2 * t + 1, rows, :] = src[2 * t + 1]
-            tile(t)
-            return 0
-
-        lax.fori_loop(0, CHUNK, one, 0, unroll=2)
-
-    copies = [pack(0, own)]
+                for e in range(CHUNK):
+                    ext[2 * first + e, rows, :] = src[2 * first + e]
+
+        @pl.when(p == NCHUNK)
+        def _():
+            face_rows()
+
+        tile(first)
+        tile(first + 1)
+        return 0
+
+    pack(0, own)
     prod[EXT] = jnp.zeros((OFFSETS * LOC, BLOCK), F32)
     ext[EXT] = jnp.zeros((CH, BLOCK), BF16)
     low = lax.broadcasted_iota(jnp.int32, (LOC, BLOCK), 1) < LOC
-    for p in range(WPAD // BLOCK):
+
+    def columns(p, _):
         for h in range(2):
             cols = pl.ds(h * BLOCK, BLOCK)
-            first = w_ref[pl.ds(2 * p * LOC, LOC), cols].astype(F32)
-            if 2 * p + 1 < OFFSETS:
-                second = w_ref[pl.ds((2 * p + 1) * LOC, LOC), cols].astype(F32)
-            else:
-                second = jnp.zeros((LOC, BLOCK), F32)
-            put = pl.ds(p * BLOCK, BLOCK)
+            first = w_ref[pl.ds(pl.multiple_of(2 * p * LOC, LOC), LOC), cols].astype(F32)
+            row = jnp.minimum(2 * p + 1, OFFSETS - 1) * LOC
+            second = w_ref[pl.ds(pl.multiple_of(row, LOC), LOC), cols].astype(F32)
+            second = jnp.where(2 * p + 1 < OFFSETS, second, 0.0)
+            put = pl.ds(pl.multiple_of(p * BLOCK, BLOCK), BLOCK)
             parts_ref[2 * h, :, put] = jnp.where(low, first, pltpu.roll(second, LOC, 1)).astype(BF16)
             parts_ref[2 * h + 1, :, put] = jnp.where(low, pltpu.roll(first, LOC, 1), second).astype(BF16)
-    gather.forward(0)
+        return 0
+
+    lax.fori_loop(0, WPAD // BLOCK, columns, 0)
+    gather.advance(0)
     target = pair_targets(map_ref)
-    gather.forward(1)
+    gather.advance(1)
     rank = pair_ranks(map_ref, target)
-    gather.forward(2)
+    gather.advance(2)
     meta_ref[...] = sort_pairs(target, rank)
-    gather.forward(3)
-    for i in range(NFWD - 1):
-        gather.wait_part(i)
-        part_tiles(i)
-    gather.wait_part(NFWD - 1)
-    copies.append(pack(1, from_dn))
-    copies.append(pack(2, from_up))
-    copies.append(pack(3, opp))
-    part_tiles(NFWD - 1)
-    keep_below = jnp.where(b > 0, 1.0, 0.0)
-    keep_above = jnp.where(b < NBOX - 1, 1.0, 0.0)
-    for r, (r_abs, _) in enumerate(quarters):
-        up, dn = copies[r]
-        up.wait_recv()
-        dn.wait_recv()
-        rows = rows_of(r_abs)
-        for s in range(SLOTS):
-            ext[BLOCKS + s, rows, :] = (fin[r, 0, s].astype(F32) * keep_below).astype(BF16)
-            ext[BLOCKS + SLOTS + s, rows, :] = (fin[r, 1, s].astype(F32) * keep_above).astype(BF16)
-
-    def face_tile(t, _):
-        tile(t)
-        return 0
-
-    lax.fori_loop(BLOCKS // 2, EXT // 2, face_tile, 0, unroll=2)
-
+    gather.advance(3)
+    gather.start_far()
+    gather.wait_near()
+    pack(1, from_dn)
+    pack(2, from_up)
+    lax.fori_loop(0, EXT // 4, two_tiles, 0)
     leave = pltpu.make_async_copy(ext, ext_to, esem)
     leave.start()
 
@@ -298,9 +345,9 @@
     sum_ref[1] = s
     leave.wait()
     gather.wait_sends()
-    for up, dn in copies:
-        up.wait_send()
-        dn.wait_send()
+    for r in range(4):
+        for c in face_copies(r):
+            c.wait_send()
 
 
 def conv_call(send, kmap, features, occ, w):

time: 115 us -> 113 us (0.983)
  Pallas kernels: 115 us -> 112 us
    pallas_call x1, Pallas kernels: 40 us -> 35.8 us  [conv_call(): pl.pallas_call(conv_kernel, out_shape=(jax.ShapeDtypeStruct((BLOCKS, LOC,...]
    pallas_call x1, Pallas kernels: 70.6 us -> 72.4 us  [norm_call(): pl.pallas_call(norm_kernel, out_shape=(jax.ShapeDtypeStruct((LOC, BLOCKS...]
where the time goes in v6:
time: 113 us
  Pallas kernels  112 us (99%)
    pallas_call x1, Pallas kernels, norm_call(): pl.pallas_call(norm_kernel, out_shape=(jax.ShapeDtypeStruct((LOC, BLOCKS...  72.4 us
    pallas_call x1, Pallas kernels, conv_call(): pl.pallas_call(conv_kernel, out_shape=(jax.ShapeDtypeStruct((BLOCKS, LOC,...  35.8 us
    pallas_call x1, Pallas kernels, emit_call(): pl.pallas_call(emit_kernel, out_shape=(whole, whole, jax.ShapeDtypeStruct...  4.01 us

profile of v6, /device:TPU:1, one launch (start us, length us, event | category | flops | bytes accessed | tf_op | source)
XLA Modules:
  0.0 112.9 jit_solution(2501894852047989693)
XLA Ops:
  0.6 35.8 %conv.1 = (f32[32,64,128]{2,1,0:T(8,128)}, f32[2,64,128]{2,1,0:T(8,128)}, bf16[49,256,128]{2,1,0:T(8,128)(2,1)}, bf16[4,64,1792]{2,1,0:T(8,128)(2,1)}, s32[16,128]{1,0:T(8,128)}) custom-call(s32[1,2,8]{2,1,0:T(2,128)} %send_ref.5, s32[27,1,32]{2,1,0:T(1,128)} %bitcast.11, bf16[64,4096]{1,0:T(8,128)(2,1)} %feat_ref.1, s32[32,1,128]{2,1,0:T(1,128)} %bitcast.8, ...), custom_call_target="tpu_custom_call" | custom-call | tf_op jit(solution)/shard_map/conv/pallas_call | solution.py:357
  36.5 72.4 %norm.1 = (bf16[64,4096]{1,0:T(8,128)(2,1)}, f32[32,64,128]{2,1,0:T(8,128)}, bf16[2,8,64,128]{3,2,1,0:T(8,128)(2,1)}, bf16[4,2,512,128]{3,2,1,0:T(8,128)(2,1)}, f32[1,128]{1,0:T(1,128)}) custom-call(s32[1,2,8]{2,1,0:T(2,128)} %send_ref.5, s32[27,1,32]{2,1,0:T(1,128)} %bitcast.12, s32[16,128]{1,0:T(8,128)} %get-tuple-element.20.meta_ref, ...), custom_call_target="tpu_custom_call" | custom-call | tf_op jit(solution)/shard_map/norm/pallas_call | solution.py:792
  108.9 4.0 %emit.1 = (bf16[64,4096]{1,0:T(8,128)(2,1)}, bf16[64,4096]{1,0:T(8,128)(2,1)}, f32[27,64,256]{2,1,0:T(8,128)}, f32[1,64]{1,0:T(1,128)}, f32[1,64]{1,0:T(1,128)}) custom-call(s32[1,2,8]{2,1,0:T(2,128)} %send_ref.5, bf16[64,4096]{1,0:T(8,128)(2,1)} %get-tuple-element.25.out_ref, f32[32,64,128]{2,1,0:T(8,128)} %get-tuple-element.26.eg_ref, ...), custom_call_target="tpu_custom_call" | custom-call | tf_op jit(solution)/shard_map/emit/pallas_call | solution.py:878

commit v7 on v6

--- a/solution.py
+++ b/solution.py
@@ -54,7 +54,7 @@
     barrier = pltpu.get_barrier_semaphore()
     for dev in devs:
         pl.semaphore_signal(barrier, inc=1, device_id=dev, device_id_type=MESH)
-    pl.semaphore_wait(barrier, len(devs))
+    return lambda: pl.semaphore_wait(barrier, len(devs))
 
 
 def occ_of(occ_ref, j):
@@ -231,13 +231,15 @@
     gather = YGather(own, from_dn, from_up, opp, ysend, yrecv)
     quarters = ((q, own), (lax.rem(q + 3, 4), from_dn), (lax.rem(q + 1, 4), from_up), (lax.rem(q + 2, 4), opp))
 
+    all_here = greet([gather.up, gather.dn, above, below])
+
     def mask(e, _):
         x = feat_ref[:, pl.ds(pl.multiple_of(e * BLOCK, BLOCK), BLOCK)].astype(F32)
         own[e] = (x * occ_of(occ_ref, e)).astype(BF16)
         return 0
 
     lax.fori_loop(0, BLOCKS, mask, 0)
-    greet([gather.up, gather.dn, above, below])
+    all_here()
     gather.start_near()
 
     def pack(r, src):
@@ -455,11 +457,13 @@
     shift_ref,
     ext_from,
     parts_ref,
-    out_ref,
-    eg,
+    out_to,
+    eg_to,
     fin,
     res,
     stat_ref,
+    out_ref,
+    eg,
     grad_ref,
     ext_ref,
     relay,
@@ -509,12 +513,13 @@
     for c in loads:
         c.start()
 
+    all_here = greet([gather.up, gather.dn] + near + far + [above, below])
     count = jnp.sum(occ_ref[...].astype(F32), axis=0)
     count = jnp.broadcast_to(jnp.sum(count, axis=1, keepdims=True), (1, BLOCK))
     row = to_row(sum_ref[0], sum_ref[1])
     sub = lax.broadcasted_iota(jnp.int32, (2, BLOCK), 0)
     pay = jnp.where(sub == 0, row, count)
-    greet([gather.up, gather.dn] + near + far + [above, below])
+    all_here()
     wcopies = []
 
     def wcopy(src, dst, i, dev):
@@ -577,6 +582,8 @@
 
     zero = jnp.zeros((LOC, BLOCK), F32)
     a, s = lax.fori_loop(0, BLOCKS, fwd, (zero, zero))
+    leave = [pltpu.make_async_copy(out_ref, out_to, lsem.at[2]), pltpu.make_async_copy(eg, eg_to, lsem.at[3])]
+    leave[0].start()
     row = to_row(a, s)
 
     def turn(step):
@@ -772,6 +779,7 @@
         return 0
 
     lax.fori_loop(0, BLOCKS, keep, 0)
+    leave[1].start()
     step4(2)
     step4(3)
     step5(1)
@@ -781,6 +789,8 @@
     step5(3)
     for h in range(PARTS):
         arrive(h)
+    for c in leave:
+        c.wait()
     gather.wait_sends()
     for c in sent:
         c.wait_send()
@@ -799,8 +809,10 @@
             jax.ShapeDtypeStruct((1, BLOCK), F32),
         ),
         in_specs=[SMEM] * 3 + [VMEM, VMEM, ANY, VMEM, VMEM, VMEM, ANY, VMEM],
-        out_specs=(VMEM,) * 5,
+        out_specs=(ANY, ANY, VMEM, VMEM, VMEM),
         scratch_shapes=[
+            pltpu.VMEM((LOC, BLOCKS * BLOCK), BF16),
+            pltpu.VMEM((BLOCKS, LOC, BLOCK), F32),
             pltpu.VMEM((LOC, BLOCKS * BLOCK), BF16),
             pltpu.VMEM((EXT + 1, CH, BLOCK), BF16),
             pltpu.VMEM((2, LOC // 2, WPAD), BF16),
@@ -833,7 +845,7 @@
             dma((2,)),
             dma((PARTS, 22)),
             dma((PARTS, 22)),
-            dma((2,)),
+            dma((4,)),
         ],
         compiler_params=params(2),
         name="norm",

time: 113 us -> 112 us (level)
  no operation moved by 1% of the time
where the time goes in v7:
time: 112 us
  Pallas kernels  111 us (99%)
    pallas_call x1, Pallas kernels, norm_call(): pl.pallas_call(norm_kernel, out_shape=(jax.ShapeDtypeStruct((LOC, BLOCKS...  71.9 us
    pallas_call x1, Pallas kernels, conv_call(): pl.pallas_call(conv_kernel, out_shape=(jax.ShapeDtypeStruct((BLOCKS, LOC,...  35.5 us
    pallas_call x1, Pallas kernels, emit_call(): pl.pallas_call(emit_kernel, out_shape=(whole, whole, jax.ShapeDtypeStruct...  4.01 us

profile of v7, /device:TPU:1, one launch (start us, length us, event | category | flops | bytes accessed | tf_op | source)
XLA Modules:
  0.0 112.1 jit_solution(68472338052943692)
XLA Ops:
  0.6 35.5 %conv.1 = (f32[32,64,128]{2,1,0:T(8,128)}, f32[2,64,128]{2,1,0:T(8,128)}, bf16[49,256,128]{2,1,0:T(8,128)(2,1)}, bf16[4,64,1792]{2,1,0:T(8,128)(2,1)}, s32[16,128]{1,0:T(8,128)}) custom-call(s32[1,2,8]{2,1,0:T(2,128)} %send_ref.5, s32[27,1,32]{2,1,0:T(1,128)} %bitcast.11, bf16[64,4096]{1,0:T(8,128)(2,1)} %feat_ref.1, s32[32,1,128]{2,1,0:T(1,128)} %bitcast.8, ...), custom_call_target="tpu_custom_call" | custom-call | tf_op jit(solution)/shard_map/conv/pallas_call | solution.py:359
  36.2 71.9 %norm.1 = (bf16[64,4096]{1,0:T(8,128)(2,1)}, f32[32,64,128]{2,1,0:T(8,128)}, bf16[2,8,64,128]{3,2,1,0:T(8,128)(2,1)}, bf16[4,2,512,128]{3,2,1,0:T(8,128)(2,1)}, f32[1,128]{1,0:T(1,128)}) custom-call(s32[1,2,8]{2,1,0:T(2,128)} %send_ref.5, s32[27,1,32]{2,1,0:T(1,128)} %bitcast.12, s32[16,128]{1,0:T(8,128)} %get-tuple-element.20.meta_ref, ...), custom_call_target="tpu_custom_call" | custom-call | tf_op jit(solution)/shard_map/norm/pallas_call | solution.py:802
  108.0 4.0 %emit.1 = (bf16[64,4096]{1,0:T(8,128)(2,1)}, bf16[64,4096]{1,0:T(8,128)(2,1)}, f32[27,64,256]{2,1,0:T(8,128)}, f32[1,64]{1,0:T(1,128)}, f32[1,64]{1,0:T(1,128)}) custom-call(s32[1,2,8]{2,1,0:T(2,128)} %send_ref.5, bf16[64,4096]{1,0:T(8,128)(2,1)} %get-tuple-element.25.out_ref, f32[32,64,128]{2,1,0:T(8,128)} %get-tuple-element.26.eg_ref, ...), custom_call_target="tpu_custom_call" | custom-call | tf_op jit(solution)/shard_map/emit/pallas_call | solution.py:890

commit v8 on v7

--- a/solution.py
+++ b/solution.py
@@ -342,7 +342,7 @@
         return a + o, s + o * acc
 
     zero = jnp.zeros((LOC, BLOCK), F32)
-    a, s = lax.fori_loop(0, BLOCKS, out, (zero, zero), unroll=2)
+    a, s = lax.fori_loop(0, BLOCKS, out, (zero, zero), unroll=4)
     sum_ref[0] = a
     sum_ref[1] = s
     leave.wait()
@@ -581,7 +581,7 @@
         return a + rg, s + rg * nd
 
     zero = jnp.zeros((LOC, BLOCK), F32)
-    a, s = lax.fori_loop(0, BLOCKS, fwd, (zero, zero))
+    a, s = lax.fori_loop(0, BLOCKS, fwd, (zero, zero), unroll=2)
     leave = [pltpu.make_async_copy(out_ref, out_to, lsem.at[2]), pltpu.make_async_copy(eg, eg_to, lsem.at[3])]
     leave[0].start()
     row = to_row(a, s)
@@ -599,14 +599,14 @@
     stat_ref[...] = tot
     sg, gg = to_cols(tot)
     scale = inv * gain
-    sgm = sg / n_vox
+    sgm, ggm = sg / n_vox, gg / n_vox
 
     def bwd(j, _):
         nd, rg = run[2 * j], run[2 * j + 1]
-        own[j] = (occ_of(occ_ref, j) * scale * (rg - sgm - nd * gg / n_vox)).astype(BF16)
+        own[j] = (occ_of(occ_ref, j) * scale * (rg - sgm - nd * ggm)).astype(BF16)
         return 0
 
-    lax.fori_loop(0, BLOCKS, bwd, 0)
+    lax.fori_loop(0, BLOCKS, bwd, 0, unroll=2)
     gather.start()
 
     def kterm(k, _):
@@ -778,7 +778,7 @@
         eg[d] = total(d)
         return 0
 
-    lax.fori_loop(0, BLOCKS, keep, 0)
+    lax.fori_loop(0, BLOCKS, keep, 0, unroll=2)
     leave[1].start()
     step4(2)
     step4(3)

time: 112 us -> 110 us (0.982)
  Pallas kernels: 111 us -> 109 us
    pallas_call x1, Pallas kernels: 71.9 us -> 69.8 us  [norm_call(): pl.pallas_call(norm_kernel, out_shape=(jax.ShapeDtypeStruct((LOC, BLOCKS...]
where the time goes in v8:
time: 110 us
  Pallas kernels  109 us (99%)
    pallas_call x1, Pallas kernels, norm_call(): pl.pallas_call(norm_kernel, out_shape=(jax.ShapeDtypeStruct((LOC, BLOCKS...  69.8 us
    pallas_call x1, Pallas kernels, conv_call(): pl.pallas_call(conv_kernel, out_shape=(jax.ShapeDtypeStruct((BLOCKS, LOC,...  35.4 us
    pallas_call x1, Pallas kernels, emit_call(): pl.pallas_call(emit_kernel, out_shape=(whole, whole, jax.ShapeDtypeStruct...  4.01 us

profile of v8, /device:TPU:1, one launch (start us, length us, event | category | flops | bytes accessed | tf_op | source)
XLA Modules:
  0.0 109.8 jit_solution(5539919901856345867)
XLA Ops:
  0.6 35.4 %conv.1 = (f32[32,64,128]{2,1,0:T(8,128)}, f32[2,64,128]{2,1,0:T(8,128)}, bf16[49,256,128]{2,1,0:T(8,128)(2,1)}, bf16[4,64,1792]{2,1,0:T(8,128)(2,1)}, s32[16,128]{1,0:T(8,128)}) custom-call(s32[1,2,8]{2,1,0:T(2,128)} %send_ref.5, s32[27,1,32]{2,1,0:T(1,128)} %bitcast.11, bf16[64,4096]{1,0:T(8,128)(2,1)} %feat_ref.1, s32[32,1,128]{2,1,0:T(1,128)} %bitcast.8, ...), custom_call_target="tpu_custom_call" | custom-call | tf_op jit(solution)/shard_map/conv/pallas_call | solution.py:359
  36.1 69.8 %norm.1 = (bf16[64,4096]{1,0:T(8,128)(2,1)}, f32[32,64,128]{2,1,0:T(8,128)}, bf16[2,8,64,128]{3,2,1,0:T(8,128)(2,1)}, bf16[4,2,512,128]{3,2,1,0:T(8,128)(2,1)}, f32[1,128]{1,0:T(1,128)}) custom-call(s32[1,2,8]{2,1,0:T(2,128)} %send_ref.5, s32[27,1,32]{2,1,0:T(1,128)} %bitcast.12, s32[16,128]{1,0:T(8,128)} %get-tuple-element.20.meta_ref, ...), custom_call_target="tpu_custom_call" | custom-call | tf_op jit(solution)/shard_map/norm/pallas_call | solution.py:802
  105.8 4.0 %emit.1 = (bf16[64,4096]{1,0:T(8,128)(2,1)}, bf16[64,4096]{1,0:T(8,128)(2,1)}, f32[27,64,256]{2,1,0:T(8,128)}, f32[1,64]{1,0:T(1,128)}, f32[1,64]{1,0:T(1,128)}) custom-call(s32[1,2,8]{2,1,0:T(2,128)} %send_ref.5, bf16[64,4096]{1,0:T(8,128)(2,1)} %get-tuple-element.25.out_ref, f32[32,64,128]{2,1,0:T(8,128)} %get-tuple-element.26.eg_ref, ...), custom_call_target="tpu_custom_call" | custom-call | tf_op jit(solution)/shard_map/emit/pallas_call | solution.py:890
